TPU v7x, 256 devices: a whole 4x4x8 slice. The times are simulated.
256 devices in a mesh: member: 8 (over y_hi, x), dp: 32 (over z, y_lo, core).
Axes of the slice: x: 4, y: 4 (y_hi: 2, y_lo: 2; y = y_hi * 2 + y_lo), z: 8, core: 2. Of those that a mesh axis runs over, the one named last changes fastest.
Arguments:
- inputs: bfloat16 [8, 4096, 896], P('member', 'dp'), may hold values from -6 to 6
- cotangent: bfloat16 [8, 4096, 896], P('member', 'dp'), may hold values from -6 to 6
- counts: int32 [8, 4096], P('member', 'dp'), may hold values from 0 to 3
- pre_hidden: bfloat16 [8, 15360, 4096], P('member', 'dp'), may hold values from -6 to 6
- pre_out: bfloat16 [8, 4096, 896], P('member', 'dp'), may hold values from -6 to 6
- w_in: bfloat16 [15360, 896], P('dp'), may hold values from -0.1875 to 0.1875
- w_out: bfloat16 [15360, 896], P('dp'), may hold values from -0.046875 to 0.046875
- r_in: float32 [8, 896], P('member'), may hold values from 0.1 to 1.9
- s_in: float32 [8, 15360], P('member', 'dp'), may hold values from 0.1 to 1.9
- r_out: float32 [8, 15360], P('member', 'dp'), may hold values from 0.1 to 1.9
- s_out: float32 [8, 896], P('member'), may hold values from 0.1 to 1.9
Outputs:
- grad_inputs: float32 [8, 4096, 896], P('member', 'dp')
- grad_w_in: float32 [15360, 896], P('dp')
- grad_w_out: float32 [15360, 896], P('dp')
- grad_r_in: float32 [8, 896], P('member')
- grad_s_in: float32 [8, 15360], P('member', 'dp')
- grad_r_out: float32 [8, 15360], P('member', 'dp')
- grad_s_out: float32 [8, 896], P('member')
All inputs are finite; a program needn't handle non-finite values.
Results may differ from a plain program's by a relative error of at most 0.005.
Values may be sent and summed in bfloat16 or wider, within the bound.
A program may use at most 128 MiB of HBM per device.

v0:
```python
import jax
import jax.numpy as jnp
from jax import lax
from jax.sharding import PartitionSpec as P


def gelu_pair(value):
    normal_cdf = 0.5 * (1.0 + jax.scipy.special.erf(value * 0.7071067811865476))
    slope = normal_cdf + value * jnp.exp(-0.5 * value * value) * 0.3989422804014327
    return (value * normal_cdf, slope)


def per_device(
    inputs, cotangent, counts, pre_hidden, pre_out, w_in, w_out, r_in, s_in, r_out, s_out
):
    all_rows = pre_hidden.shape[2]
    member_count = lax.axis_size("member")
    token_scale = 1.0 / jnp.sqrt(jnp.float32(all_rows))
    weight_scale = 1.0 / jnp.sqrt(jnp.float32(member_count * all_rows))
    weighted = cotangent[0].astype(jnp.float32) * counts[0].astype(jnp.float32)[:, None]
    out_part = jnp.sum(weighted * pre_out[0].astype(jnp.float32), axis=0)
    grad_z = (weighted * s_out[0][None, :]).astype(jnp.bfloat16)
    scaled_in = (inputs[0].astype(jnp.float32) * r_in[0][None, :]).astype(jnp.bfloat16)
    in_all, z_all = (
        lax.all_gather(scaled_in, "dp", axis=0, tiled=True),
        lax.all_gather(grad_z, "dp", axis=0, tiled=True),
    )
    pre_f = pre_hidden[0].astype(jnp.float32)
    act = pre_f * s_in[0][:, None]
    gelu_val, slope = gelu_pair(act)
    hidden = (gelu_val * r_out[0][:, None]).astype(jnp.bfloat16)
    grad_u = lax.dot_general(
        w_out, z_all, (((1,), (1,)), ((), ())), preferred_element_type=jnp.float32
    )
    grad_wo = jnp.dot(hidden, z_all, preferred_element_type=jnp.float32)
    grad_ro = jnp.sum(grad_u * gelu_val, axis=1) * token_scale
    grad_act = grad_u * r_out[0][:, None] * slope
    grad_si = jnp.sum(grad_act * pre_f, axis=1) * token_scale
    grad_pre = (grad_act * s_in[0][:, None]).astype(jnp.bfloat16)
    grad_h = lax.psum_scatter(
        lax.dot_general(
            grad_pre, w_in, (((0,), (0,)), ((), ())), preferred_element_type=jnp.float32
        ),
        "dp",
        scatter_dimension=0,
        tiled=True,
    )
    grad_wi = jnp.dot(grad_pre, in_all, preferred_element_type=jnp.float32)
    grad_x = grad_h * r_in[0][None, :]
    in_part = jnp.sum(grad_h * inputs[0].astype(jnp.float32), axis=0)
    in_total, out_total = lax.psum((in_part, out_part), "dp")
    grad_wi, grad_wo = lax.psum((grad_wi, grad_wo), "member")
    return (
        grad_x[None],
        grad_wi * weight_scale,
        grad_wo * weight_scale,
        (in_total * token_scale)[None],
        grad_si[None],
        grad_ro[None],
        (out_total * token_scale)[None],
    )


def solution(mesh):
    return jax.shard_map(
        per_device,
        mesh=mesh,
        in_specs=(
            P("member", "dp", None),
            P("member", "dp", None),
            P("member", "dp"),
            P("member", "dp", None),
            P("member", "dp", None),
            P("dp", None),
            P("dp", None),
            P("member", None),
            P("member", "dp"),
            P("member", "dp"),
            P("member", None),
        ),
        out_specs=(
            P("member", "dp", None),
            P("dp", None),
            P("dp", None),
            P("member", None),
            P("member", "dp"),
            P("member", "dp"),
            P("member", None),
        ),
        check_vma=False,
    )
```

profile of v0, /device:TPU:16, one launch (start us, length us, event | category | flops | bytes accessed | tf_op | source)
XLA Modules:
  0.0 476.3 jit_solution(11376833055882631518)
XLA Ops:
  7.2 0.0 copy-start
  7.2 0.0 all-gather.3.cloned.1.call-start
  7.2 0.7 convert_bitcast_fusion
  8.0 0.7 reduce
  8.7 1.9 fusion.18
  10.6 0.0 all-gather.3.cloned.1.call-update
  10.6 0.0 reduce-scatter.2.cloned.1.call-start
  10.6 74.0 %all-gather.3.cloned.1.call-done = bf16[4096,896]{1,0:T(8,128)(2,1)} async-done(((bf16[128,896]{1,0:T(8,128)(2,1)}), bf16[4096,896]{1,0:T(8,128)(2,1)}) %all-gather.3.cloned.1.call-update) | async-done | bytes 7340048 | tf_op jit(solution)/shard_map/all_gather | solution.py:26
  84.7 0.0 copy-done
  84.7 12.2 %fusion.11 = (f32[480]{0:T(512)S(1)}, f32[480]{0:T(512)S(1)}, f32[480,4096]{1,0:T(8,128)S(1)}, f32[480,4096]{1,0:T(8,128)}) fusion(bf16[1,480,4096]{2,1,0:T(8,128)(2,1)} %param.14, f32[480]{0:T(512)} %bitcast.44, f32[480]{0:T(512)} %bitcast.50, bf16[4096,896]{1,0:T(8,128)(2,1)} %all-gather.3.cloned.1.call-done, bf16[480,896]{1,0:T(8,128)(2,1)S(1)} %copy-done), kind=kOutput, calls=%fused_computation.16 | convolution fusion | flops 3556637696 | bytes 27868672 | tf_op jit(solution)/shard_map/dot_general | solution.py:32
  96.9 3.2 copy-done.1
  100.1 0.0 copy-done.2
  100.1 0.0 copy-done.4
  100.1 8.0 %fusion.22 = f32[4096,896]{1,0:T(8,128)} fusion(bf16[480,896]{1,0:T(8,128)(2,1)S(1)} %copy-done.2, f32[480,4096]{1,0:T(8,128)S(1)} %get-tuple-element.13, f32[480]{0:T(512)S(1)} %bitcast.45), kind=kOutput, calls=%fused_computation.41 | convolution fusion | flops 3527147520 | bytes 23406464 | tf_op jit(solution)/shard_map/dot_general | solution.py:41
  108.1 0.0 reduce-scatter.2.cloned.1.call-update
  108.1 0.0 all-gather.5.cloned.1.call-start
  108.2 0.6 copy-done.5
  108.8 167.0 %reduce-scatter.2.cloned.1.call-done = f32[128,896]{1,0:T(8,128)} async-done(((f32[4096,896]{1,0:T(8,128)}), f32[128,896]{1,0:T(8,128)}) %reduce-scatter.2.cloned.1.call-update) | async-done | bytes 458768 | tf_op jit(solution)/shard_map/reduce_scatter | solution.py:40
  275.8 0.0 copy-done.3
  275.8 1.9 fusion.17
  277.7 0.0 all-gather.5.cloned.1.call-update
  277.7 0.2 all-reduce.4.cloned.1.call-start
  278.0 12.0 %fusion.12 = f32[480,896]{1,0:T(8,128)} fusion(bf16[4096,896]{1,0:T(8,128)(2,1)} %all-gather.3.cloned.1.call-done, f32[480,4096]{1,0:T(8,128)} %get-tuple-element.14, bf16[1,480,4096]{2,1,0:T(8,128)(2,1)} %param.14, f32[480]{0:T(512)S(1)} %bitcast.46, f32[480]{0:T(512)S(1)} %bitcast.51), kind=kOutput, calls=%fused_computation.19 | convolution fusion | flops 3533045760 | bytes 20860672 | tf_op jit(solution)/shard_map/dot_general | solution.py:35
  290.0 59.3 %all-gather.5.cloned.1.call-done = bf16[4096,896]{1,0:T(8,128)(2,1)} async-done(((bf16[128,896]{1,0:T(8,128)(2,1)}), bf16[4096,896]{1,0:T(8,128)(2,1)}) %all-gather.5.cloned.1.call-update) | async-done | bytes 7340048 | tf_op jit(solution)/shard_map/all_gather | solution.py:25
  349.3 10.8 %fusion.21 = f32[480,896]{1,0:T(8,128)} fusion(bf16[4096,896]{1,0:T(8,128)(2,1)} %all-gather.5.cloned.1.call-done, f32[480,4096]{1,0:T(8,128)} %copy-done.1, f32[480]{0:T(512)S(1)} %bitcast.47), kind=kOutput, calls=%fused_computation.40 | convolution fusion | flops 3527147520 | bytes 16926592 | tf_op jit(solution)/shard_map/dot_general | solution.py:48
  360.1 0.0 all-reduce.4.cloned.1.call-update
  360.1 0.6 broadcast_multiply_fusion.4
  360.7 63.3 %all-reduce = (f32[896]{0:T(1024)S(1)}, f32[896]{0:T(1024)S(1)}) all-reduce(f32[896]{0:T(1024)S(1)} %get-tuple-element.15, f32[896]{0:T(1024)S(1)} %get-tuple-element.18), channel_id=1, replica_groups=mesh['member'=8,'dp'=32] {'dp'}, use_global_device_ids=true, to_apply=%region_4.0 | all-reduce | flops 1792 | bytes 14336 | tf_op jit(solution)/shard_map/psum | solution.py:51
  424.0 0.6 broadcast_in_dim.14
  424.6 0.6 broadcast_in_dim.13
  425.1 40.6 %all-reduce.4.cloned.1.call-done = (f32[480,896]{1,0:T(8,128)}, f32[480,896]{1,0:T(8,128)}) async-done(((f32[480,896]{1,0:T(8,128)}, f32[480,896]{1,0:T(8,128)}), (f32[480,896]{1,0:T(8,128)}, f32[480,896]{1,0:T(8,128)})) %all-reduce.4.cloned.1.call-update) | async-done | bytes 3440656 | tf_op jit(solution)/shard_map/psum | solution.py:52
  465.7 4.0 broadcast_multiply_fusion
  (9 shorter events, 0.0 us)
Async XLA Ops:
  7.2 77.5 %copy-start = (bf16[480,896]{1,0:T(8,128)(2,1)S(1)}, bf16[480,896]{1,0:T(8,128)(2,1)}, u32[]{:S(2)}) copy-start(bf16[480,896]{1,0:T(8,128)(2,1)} %param.17) | copy-start | bytes 2580484
  7.2 77.5 %all-gather.3.cloned.1.call-start = ((), (), s32[]{:S(2)}) async-start(), calls=%async_computation.1 | async-start | bytes 7569408 | tf_op jit(solution)/shard_map/all_gather | solution.py:26
  10.6 265.2 %reduce-scatter.2.cloned.1.call-start = ((), (), s32[]{:S(2)}) async-start(), calls=%async_computation.2 | async-start | bytes 15138816 | tf_op jit(solution)/shard_map/reduce_scatter | solution.py:40
  84.7 15.4 %copy-start.2 = (bf16[480,896]{1,0:T(8,128)(2,1)S(1)}, bf16[480,896]{1,0:T(8,128)(2,1)}, u32[]{:S(2)}) copy-start(bf16[480,896]{1,0:T(8,128)(2,1)} %param.16) | copy-start | bytes 2580484
  84.7 15.4 %copy-start.4 = (f32[1,480]{1,0:T(1,128)S(1)}, f32[1,480]{1,0:T(1,128)}, u32[]{:S(2)}) copy-start(f32[1,480]{1,0:T(1,128)} %param.19) | copy-start | bytes 5764
  96.9 3.2 copy-start.1
  108.1 0.7 copy-start.5
  108.1 167.7 %copy-start.3 = (bf16[1,128,896]{2,1,0:T(8,128)(2,1)S(1)}, bf16[1,128,896]{2,1,0:T(8,128)(2,1)}, u32[]{:S(2)}) copy-start(bf16[1,128,896]{2,1,0:T(8,128)(2,1)} %param.11) | copy-start | bytes 688132
  108.1 169.9 %copy-start.6 = (f32[1,480]{1,0:T(1,128)S(1)}, f32[1,480]{1,0:T(1,128)}, u32[]{:S(2)}) copy-start(f32[1,480]{1,0:T(1,128)} %param.20) | copy-start | bytes 5764
  108.1 241.2 %all-gather.5.cloned.1.call-start = ((), (), s32[]{:S(2)}) async-start(), calls=%async_computation.3 | async-start | bytes 7569408 | tf_op jit(solution)/shard_map/all_gather | solution.py:25
  277.7 188.0 %all-reduce.4.cloned.1.call-start = ((), (), s32[]{:S(2)}) async-start(), calls=%async_computation.4 | async-start | bytes 6881280 | tf_op jit(solution)/shard_map/psum | solution.py:52
Sparse Core Ops, SparseCore 0:
  10.7 73.9 all-gather.2
  108.3 167.4 reduce-scatter.1
  278.2 71.0 all-gather.4
  360.2 105.4 all-reduce.3
where the time goes:
time: 479 us; the launch traced here: 476 us
  waiting for transfers between devices  341 us (71%)
  blocking collectives  63.3 us (13%)
  matrix products  43 us (9%)
  between operations  13.8 us (3%)
  other arithmetic  9.91 us (2%)
  local copies, waits for them, and re-layouts  4.95 us (1%)
    reduce_scatter x1, waiting for transfers between devices, per_device(): lax.psum_scatter(lax.dot_general(grad_pre, w_in, (((0,), (0,)), ((), ()))...  167 us
    all_gather x1, waiting for transfers between devices, per_device(): lax.all_gather(grad_z, 'dp', axis=0, tiled=True)  74 us
    psum x1, blocking collectives, per_device(): in_total, out_total = lax.psum((in_part, out_part), 'dp')  63.3 us
    all_gather x1, waiting for transfers between devices, per_device(): lax.all_gather(scaled_in, 'dp', axis=0, tiled=True)  59.3 us
    psum x1, waiting for transfers between devices, per_device(): grad_wi, grad_wo = lax.psum((grad_wi, grad_wo), 'member')  40.6 us
    dot_general x1, matrix products, per_device(): lax.dot_general(w_out, z_all, (((1,), (1,)), ((), ())), preferred_element...  12.2 us
    dot_general x1, matrix products, per_device(): grad_wo = jnp.dot(hidden, z_all, preferred_element_type=jnp.float32)  12 us
    dot_general x1, matrix products, per_device(): grad_wi = jnp.dot(grad_pre, in_all, preferred_element_type=jnp.float32)  10.8 us
  transfers between devices with their start and end apart: 4, of which 4 were waited for; matrix products, arithmetic and copies ran while one was open for 3% of the time, Pallas kernels for 0%

commit v1 on v0

v1 whole, which is shorter than its diff:
```python
import functools

import jax
import jax.numpy as jnp
from jax import lax
from jax.experimental import pallas as pl
from jax.experimental.pallas import tpu as pltpu
from jax.sharding import PartitionSpec as P

MESH = pl.DeviceIdType.MESH
BF = jnp.bfloat16
F32 = jnp.float32

NZ = 8
TB = 128
D = 896
FB = 480
NF = 2 * FB
NH = 2

HOPS = (
    (0, (0, 0), (7, 0)), (1, (0, 0), (1, 0)), (2, (0, 0), (0, 1)),
    (0, (7, 0), (6, 0)), (1, (1, 0), (2, 0)), (2, (7, 0), (7, 1)),
    (0, (6, 0), (5, 0)), (1, (2, 0), (3, 0)), (2, (1, 0), (1, 1)),
    (0, (5, 0), (4, 0)), (1, (1, 1), (2, 1)), (2, (6, 0), (6, 1)),
    (0, (6, 1), (5, 1)), (1, (2, 1), (3, 1)), (2, (4, 0), (4, 1)),
)
ORDER = (0, 7, 1, 2, 6, 5, 3, 4)


def kernel(
    x_ref, dy_ref, cnt_ref, ph_ref, po_ref, wi_ref, wo_ref, ri_ref, si_ref, ro_ref, so_ref,
    gx_ref, gwi_ref, gwo_ref, gri_ref, gsi_ref, gro_ref, gso_ref,
    pre, slope, hid, gp, z_all, in_all, wo, wi, wt, rbuf, sbuf, acc_ro, acc_si, acc_in,
    col_s, col_r, part, sib_out, sib_in, mem_out, mem_x, mem_h, mem_all, vec_out, vec_in, vec_z,
    ring_s, ring_r, pre_l, pre_s, pre_r, w_l, w_s, w_r, col_ss, col_sr, acc_ss, acc_sr,
    sib_ss, sib_sr, x_s, x_r, h_s, h_r, all_s, all_r, vec_ss, vec_sr, vz_s, vz_r,
):
    m, d = lax.axis_index("member"), lax.axis_index("dp")
    z, y, c = d // 4, (d // 2) % 2, d % 2
    yh, x = m // 4, m % 4
    zp = (m, lax.rem(z + 1, NZ) * 4 + y * 2 + c)
    zm = (m, lax.rem(z + NZ - 1, NZ) * 4 + y * 2 + c)
    yo = (m, z * 4 + (1 - y) * 2 + c)
    co = (m, z * 4 + y * 2 + (1 - c))
    xs = [(yh * 4 + lax.rem(x + k, 4), d) for k in (1, 2, 3)]
    ho = ((1 - yh) * 4 + x, d)
    sent = []

    def send(src, dst, ss, rs, dev):
        copy = pltpu.make_async_remote_copy(
            src_ref=src, dst_ref=dst, send_sem=ss, recv_sem=rs, device_id=dev, device_id_type=MESH
        )
        copy.start()
        sent.append(copy)
        return copy

    barrier = pltpu.get_barrier_semaphore()
    for dev in (zp, zm, yo, co, ho, *xs):
        pl.semaphore_signal(barrier, inc=1, device_id=dev, device_id_type=MESH)

    local = []
    for i, s in enumerate(ORDER):
        zs = lax.rem(z + s, NZ)
        for r in range(2):
            yy = y if r == 0 else 1 - y
            col = pl.multiple_of((zs * 4 + yy * 2 + c) * TB, TB)
            copy = pltpu.make_async_copy(
                ph_ref.at[:, pl.ds(col, TB)], pre.at[s, pl.ds(0, FB), pl.ds(r * TB, TB)], pre_l.at[s, r]
            )
            copy.start()
            local.append(copy)
    w_copies = []
    for i, (src, dst) in enumerate(((wo_ref, wo), (wi_ref, wi))):
        copy = pltpu.make_async_copy(src, dst.at[pl.ds(0, FB)], w_l.at[i])
        copy.start()
        w_copies.append(copy)

    cnt = jnp.broadcast_to(cnt_ref[...].astype(F32), (TB, TB)).T
    for j in range(D // 128):
        cs = pl.ds(j * 128, 128)
        weighted = dy_ref[:, cs].astype(F32) * cnt
        z_all[0, pl.ds(0, TB), cs] = (weighted * so_ref[:, cs]).astype(BF)
        in_all[0, pl.ds(0, TB), cs] = (x_ref[:, cs].astype(F32) * ri_ref[:, cs]).astype(BF)
        vec_out[0, pl.ds(0, 1), cs] = jnp.sum(weighted * po_ref[:, cs].astype(F32), axis=0, keepdims=True)

    pl.semaphore_wait(barrier, 8)

    TP = TB // NH

    def gather_send(u, buf, step, h):
        for k in range(3 * step, 3 * step + 3):
            way, (ss, sr), (ds, dr) = HOPS[k]
            send(
                buf.at[ss, pl.ds(sr * TB + h * TP, TP)], buf.at[ds, pl.ds(dr * TB + h * TP, TP)],
                ring_s.at[u, k, h], ring_r.at[u, k, h], (zp, zm, yo)[way],
            )

    def gather_wait(u, buf, step, h):
        for k in range(3 * step, 3 * step + 3):
            way, _, (ds, dr) = HOPS[k]
            part_ref = buf.at[ds, pl.ds(dr * TB + h * TP, TP)]
            pltpu.make_async_remote_copy(
                src_ref=part_ref, dst_ref=part_ref, send_sem=ring_s.at[u, k, h], recv_sem=ring_r.at[u, k, h],
                device_id=(zp, zm, yo)[way], device_id_type=MESH,
            ).wait_recv()

    for h in range(NH):
        gather_send(0, z_all, 0, h)

    pre_in = {}
    for s in ORDER:
        zs = lax.rem(z + s, NZ)
        for r in range(2):
            yy = y if r == 0 else 1 - y
            col = pl.multiple_of((zs * 4 + yy * 2 + (1 - c)) * TB, TB)
            pre_in[s, r] = send(
                ph_ref.at[:, pl.ds(col, TB)], pre.at[s, pl.ds(FB, FB), pl.ds(r * TB, TB)],
                pre_s.at[s, r], pre_r.at[s, r], co,
            )
        if s == 0:
            col_s[pl.ds(0, FB)] = jnp.broadcast_to(si_ref[...], (128, FB)).T
            col_r[pl.ds(0, FB)] = jnp.broadcast_to(ro_ref[...], (128, FB)).T
            col_in = [
                send(b.at[pl.ds(0, FB)], b.at[pl.ds(FB, FB)], col_ss.at[i], col_sr.at[i], co)
                for i, b in enumerate((col_s, col_r))
            ]
        if s == 7:
            w_in = [
                send(src, dst.at[pl.ds(FB, FB)], w_s.at[i], w_r.at[i], co)
                for i, (src, dst) in enumerate(((wo_ref, wo), (wi_ref, wi)))
            ]
    vec_out[0, pl.ds(2, 6)] = jnp.zeros((6, D), F32)
    acc_ro[...] = jnp.zeros_like(acc_ro)
    acc_si[...] = jnp.zeros_like(acc_si)

    GT = 32

    def gelu(s, side):
        if side == 0:
            for r in range(2):
                local[2 * ORDER.index(s) + r].wait()
        else:
            for r in range(2):
                pre_in[s, r].wait_recv()

        def tile(i, _):
            rows = pl.ds(pl.multiple_of(side * FB + i * GT, GT), GT)
            sc, rc = col_s[rows], col_r[rows]
            for j in range(2):
                cs = pl.ds(j * 128, 128)
                v = pre[s, rows, cs].astype(F32) * sc
                cdf = 0.5 * (1.0 + lax.erf(v * 0.7071067811865476))
                hid[s, rows, cs] = (v * cdf * rc).astype(BF)
                pdf = jnp.exp(-0.5 * v * v) * 0.3989422804014327
                slope[s, rows, cs] = (cdf + v * pdf) * rc
            return 0

        lax.fori_loop(0, FB // GT, tile, 0)

    UT = 240

    def grad_pre(s):
        def tile(i, _):
            rows = pl.ds(pl.multiple_of(i * UT, 16), UT)
            u = lax.dot_general(wo[rows], z_all[s], (((1,), (1,)), ((), ())), preferred_element_type=F32)
            sc = col_s[rows]
            q = u * hid[s, rows].astype(F32)
            acc_ro[rows] += q[:, :128] + q[:, 128:]
            a = u * slope[s, rows]
            q = a * pre[s, rows].astype(F32)
            acc_si[rows] += q[:, :128] + q[:, 128:]
            gp[s, rows, pl.ds(0, 128)] = (a[:, :128] * sc).astype(BF)
            gp[s, rows, pl.ds(128, 128)] = (a[:, 128:] * sc).astype(BF)
            return 0

        lax.fori_loop(0, NF // UT, tile, 0)

    HT = 448

    def grad_h(s):
        def tile(i, _):
            rows = pl.ds(pl.multiple_of(i * HT, 16), HT)
            slope[s, rows] = jnp.dot(wt[rows], gp[s], preferred_element_type=F32)
            return 0

        lax.fori_loop(0, D // HT, tile, 0)

    WT = 240

    def grad_w(out, lhs, rhs, side, slots, first):
        def tile(i, _):
            rows = pl.ds(pl.multiple_of(i * WT, 16), WT)
            src = pl.ds(pl.multiple_of(side * FB + i * WT, 16), WT)
            for n, s in enumerate(slots):
                t = jnp.dot(lhs[s, src], rhs[s], preferred_element_type=F32)
                if first and n == 0:
                    out[rows] = t
                else:
                    out[rows] += t
            return 0

        lax.fori_loop(0, FB // WT, tile, 0)

    outs = (gwo_ref, gwi_ref)
    stage = {}

    def piece(xx):
        return pl.ds(pl.multiple_of(112 * xx + 16 * (xx // 2), 16), 128)

    def w_sib(g):
        sib_out[g] = part[...].astype(BF)
        stage["sib", g] = send(sib_out.at[g], sib_in.at[g], sib_ss.at[g], sib_sr.at[g], co)

    def w_x(g):
        stage["sib", g].wait_recv()
        outs[g][...] += sib_in[g].astype(F32)
        mem_out[g] = outs[g][...].astype(BF)
        stage["x", g] = [
            send(mem_out.at[g, piece(lax.rem(x + k, 4))], mem_x.at[g, k - 1], x_s.at[g, k - 1], x_r.at[g, k - 1], xs[k - 1])
            for k in (1, 2, 3)
        ]

    def w_h(g):
        for copy in stage["x", g]:
            copy.wait_recv()
        total = outs[g][piece(x)]
        for k in range(3):
            total += mem_x[g, k].astype(F32)
        mem_h[g, 0] = total.astype(BF)
        stage["h", g] = send(mem_h.at[g, 0], mem_h.at[g, 1], h_s.at[g], h_r.at[g], ho)

    def w_all(g):
        stage["h", g].wait_recv()
        mem_all[g, 0] = (mem_h[g, 0].astype(F32) + mem_h[g, 1].astype(F32)).astype(BF)
        stage["all", g] = [
            send(mem_all.at[g, 0], mem_all.at[g, k], all_s.at[g, k - 1], all_r.at[g, k - 1], xs[k - 1])
            for k in (1, 2, 3)
        ]

    def w_end(g):
        for copy in stage["all", g]:
            copy.wait_recv()
        for xx in range(4):
            rows = pl.ds(112 * xx + 16 * (xx // 2), 128)
            outs[g][rows] = mem_all[g, lax.rem(x + 4 - xx, 4)].astype(F32) * (32768.0**-0.5)

    def v_part(side, grads):
        t = jnp.sum(wi[pl.ds(side * FB, FB)].astype(F32) * grads[...], axis=0, keepdims=True)
        if side == 1:
            vec_out[0, pl.ds(1, 1)] = t
        else:
            vec_out[0, pl.ds(1, 1)] += t

    def v_pair(i, dev):
        stage["v", i] = send(vec_out.at[i], vec_in.at[i], vec_ss.at[i], vec_sr.at[i], dev)

    def v_sum(i):
        stage["v", i].wait_recv()
        t = vec_out[i] + vec_in[i]
        if i == 0:
            vec_out[1] = t
        else:
            vec_z[0] = t

    def v_send(k):
        stage["va", k] = send(vec_z.at[(8 - k) % 8], vec_z.at[7 - k], vz_s.at[0, k], vz_r.at[0, k], zp)
        if k < 3:
            stage["vb", k] = send(vec_z.at[k], vec_z.at[k + 1], vz_s.at[1, k], vz_r.at[1, k], zm)

    def v_wait(k):
        stage["va", k].wait_recv()
        if k < 3:
            stage["vb", k].wait_recv()

    def v_end():
        total = vec_z[lax.rem(NZ - z, NZ)]
        for s in range(1, NZ):
            total += vec_z[lax.rem(s + NZ - z, NZ)]
        gso_ref[...] = total[0:1] * (1.0 / 64.0)
        gri_ref[...] = total[1:2] / ri_ref[...] * (1.0 / 64.0)

    def acc_send():
        stage["acc"] = [
            send(b.at[pl.ds(FB, FB)], acc_in.at[i], acc_ss.at[i], acc_sr.at[i], co)
            for i, b in enumerate((acc_ro, acc_si))
        ]

    def acc_end():
        for copy in stage["acc"]:
            copy.wait_recv()
        t = (acc_ro[pl.ds(0, FB)] + acc_in[0]) / col_r[pl.ds(0, FB)]
        gro_ref[...] = jnp.sum(t.T, axis=0, keepdims=True) * (1.0 / 64.0)
        t = acc_si[pl.ds(0, FB)] + acc_in[1]
        gsi_ref[...] = jnp.sum(t.T, axis=0, keepdims=True) * (1.0 / 64.0)

    def transpose_w():
        w_in[1].wait_recv()
        w_copies[1].wait()
        for j in range(D // 128):
            cs = pl.ds(j * 128, 128)
            wt[cs, :] = wi[:, cs].astype(F32).T.astype(BF)

    def wait_wo():
        w_in[0].wait_recv()
        w_copies[0].wait()

    DP = D // NH

    def sum_send(step, h):
        rows = pl.ds(h * DP, DP)
        for k in range(3 * step, 3 * step + 3):
            way, _, (ds, dr) = HOPS[k]
            t = slope[ds, rows, pl.ds(dr * TB, TB)]
            for k2 in range(15):
                if HOPS[k2][1] == (ds, dr):
                    t += rbuf[k2, rows].astype(F32)
            sbuf[k, rows] = t.astype(BF)
            send(
                sbuf.at[k, rows], rbuf.at[k, rows], ring_s.at[2, k, h], ring_r.at[2, k, h], (zm, zp, yo)[way]
            )

    def sum_wait(step, h):
        for k in range(3 * step, 3 * step + 3):
            way = HOPS[k][0]
            ref = rbuf.at[k, pl.ds(h * DP, DP)]
            pltpu.make_async_remote_copy(
                src_ref=ref, dst_ref=ref, send_sem=ring_s.at[2, k, h], recv_sem=ring_r.at[2, k, h],
                device_id=(zm, zp, yo)[way], device_id_type=MESH,
            ).wait_recv()

    def col_wait():
        for copy in col_in:
            copy.wait_recv()

    def z_wait():
        for h in range(NH):
            gather_wait(0, z_all, 4, h)

    f = functools.partial
    z_work = [
        [f(gelu, 0, 0), f(gelu, 7, 0)],
        [col_wait, f(gelu, 0, 1)],
        [wait_wo, f(gelu, 7, 1), f(gelu, 1, 0)],
        [f(gelu, 1, 1), f(grad_pre, 0)],
        [f(gelu, 2, 0), f(gelu, 2, 1)],
        [f(gelu, 6, 0), f(grad_pre, 7)],
        [f(gelu, 6, 1), f(gelu, 5, 0)],
        [f(gelu, 5, 1), f(grad_pre, 1)],
        [f(gelu, 3, 0), f(gelu, 3, 1)],
        [f(gelu, 4, 0), f(gelu, 4, 1)],
    ]
    in_work = [
        [f(grad_pre, 2), transpose_w],
        [f(grad_pre, 6), f(grad_h, 6)],
        [z_wait, f(grad_pre, 5), f(grad_h, 5)],
        [f(grad_pre, 3), f(grad_h, 3)],
        [f(grad_pre, 4), f(grad_h, 4), acc_send],
        [f(grad_w, part, hid, z_all, 1, ORDER, True), f(w_sib, 0), f(grad_h, 2)],
        [f(grad_w, gwo_ref, hid, z_all, 0, ORDER, True), f(grad_h, 7)],
        [f(w_x, 0), f(grad_h, 1), f(grad_h, 0)],
        [f(grad_w, part, gp, in_all, 1, ORDER[:3], True), acc_end],
        [f(grad_w, gwi_ref, gp, in_all, 0, ORDER[:3], True), f(w_h, 0)],
    ]
    sum_work = [
        [f(grad_w, part, gp, in_all, 1, ORDER[3:], False), f(w_sib, 1), f(v_part, 1, part)],
        [f(grad_w, gwi_ref, gp, in_all, 0, ORDER[3:], False), f(v_part, 0, gwi_ref), f(v_pair, 0, co)],
        [f(w_x, 1), f(w_all, 0), f(v_sum, 0), f(v_pair, 1, yo)],
        [f(v_sum, 1), f(v_send, 0)],
        [f(w_end, 0)],
        [f(w_h, 1), f(v_wait, 0), f(v_send, 1)],
        [f(v_wait, 1), f(v_send, 2)],
        [f(v_wait, 2), f(v_send, 3)],
        [f(w_all, 1)],
        [f(v_wait, 3), v_end],
    ]

    for step in range(5):
        for h in range(NH):
            if step:
                gather_wait(0, z_all, step - 1, h)
                gather_send(0, z_all, step, h)
            for job in z_work[2 * step + h]:
                job()
    for h in range(NH):
        gather_send(1, in_all, 0, h)
    for step in range(5):
        for h in range(NH):
            if step:
                gather_wait(1, in_all, step - 1, h)
                gather_send(1, in_all, step, h)
            for job in in_work[2 * step + h]:
                job()
    for step in range(5):
        for h in range(NH):
            if step:
                sum_wait(5 - step, h)
            sum_send(4 - step, h)
            if step == 0 and h == 0:
                for hh in range(NH):
                    gather_wait(1, in_all, 4, hh)
            for job in sum_work[2 * step + h]:
                job()
    for h in range(NH):
        sum_wait(0, h)
    for j in range(D // 128):
        cs = pl.ds(j * 128, 128)
        t = slope[0, cs, pl.ds(0, TB)]
        for k in range(3):
            t += rbuf[k, cs].astype(F32)
        gx_ref[:, cs] = t.T * ri_ref[:, cs]
    w_end(1)
    for copy in sent:
        copy.wait_send()


def per_device(
    inputs, cotangent, counts, pre_hidden, pre_out, w_in, w_out, r_in, s_in, r_out, s_out
):
    vm, hbm = pl.BlockSpec(memory_space=pltpu.VMEM), pl.BlockSpec(memory_space=pl.ANY)
    dma = pltpu.SemaphoreType.DMA
    outs = pl.pallas_call(
        kernel,
        out_shape=[
            jax.ShapeDtypeStruct(shape, F32)
            for shape in ((TB, D), (FB, D), (FB, D), (1, D), (1, FB), (1, FB), (1, D))
        ],
        in_specs=[vm, vm, vm, hbm, vm, hbm, hbm, vm, vm, vm, vm],
        out_specs=[vm] * 7,
        scratch_shapes=[
            pltpu.VMEM((NZ, NF, 2 * TB), BF),
            pltpu.VMEM((NZ, NF, 2 * TB), F32),
            pltpu.VMEM((NZ, NF, 2 * TB), BF),
            pltpu.VMEM((NZ, NF, 2 * TB), BF),
            pltpu.VMEM((NZ, 2 * TB, D), BF),
            pltpu.VMEM((NZ, 2 * TB, D), BF),
            pltpu.VMEM((NF, D), BF),
            pltpu.VMEM((NF, D), BF),
            pltpu.VMEM((D, NF), BF),
            pltpu.VMEM((15, D, TB), BF),
            pltpu.VMEM((15, D, TB), BF),
            pltpu.VMEM((NF, 128), F32),
            pltpu.VMEM((NF, 128), F32),
            pltpu.VMEM((2, FB, 128), F32),
            pltpu.VMEM((NF, 128), F32),
            pltpu.VMEM((NF, 128), F32),
            pltpu.VMEM((FB, D), F32),
            pltpu.VMEM((2, FB, D), BF),
            pltpu.VMEM((2, FB, D), BF),
            pltpu.VMEM((2, FB, D), BF),
            pltpu.VMEM((2, 3, 128, D), BF),
            pltpu.VMEM((2, 2, 128, D), BF),
            pltpu.VMEM((2, 4, 128, D), BF),
            pltpu.VMEM((2, 8, D), F32),
            pltpu.VMEM((2, 8, D), F32),
            pltpu.VMEM((NZ, 8, D), F32),
            dma((3, 15, NH)), dma((3, 15, NH)),
            dma((NZ, 2)), dma((NZ, 2)), dma((NZ, 2)),
            dma((2,)), dma((2,)), dma((2,)),
            dma((2,)), dma((2,)),
            dma((2,)), dma((2,)),
            dma((2,)), dma((2,)),
            dma((2, 3)), dma((2, 3)),
            dma((2,)), dma((2,)),
            dma((2, 3)), dma((2, 3)),
            dma((2,)), dma((2,)),
            dma((2, 4)), dma((2, 4)),
        ],
        compiler_params=pltpu.CompilerParams(
            collective_id=0, has_side_effects=True, vmem_limit_bytes=63 * 2**20
        ),
    )(inputs[0], cotangent[0], counts, pre_hidden[0], pre_out[0], w_in, w_out, r_in, s_in, r_out, s_out)
    gx, gwi, gwo, gri, gsi, gro, gso = outs
    return gx[None], gwi, gwo, gri, gsi, gro, gso


def solution(mesh):
    return jax.shard_map(
        per_device,
        mesh=mesh,
        in_specs=(
            P("member", "dp", None),
            P("member", "dp", None),
            P("member", "dp"),
            P("member", "dp", None),
            P("member", "dp", None),
            P("dp", None),
            P("dp", None),
            P("member", None),
            P("member", "dp"),
            P("member", "dp"),
            P("member", None),
        ),
        out_specs=(
            P("member", "dp", None),
            P("dp", None),
            P("dp", None),
            P("member", None),
            P("member", "dp"),
            P("member", "dp"),
            P("member", None),
        ),
        check_vma=False,
    )
```

time: 479 us -> 132 us (0.28)
  waiting for transfers between devices: 341 us -> 0 us
  Pallas kernels: 0 us -> 122 us
  blocking collectives: 63.3 us -> 0 us
  matrix products: 43 us -> 0 us
  between operations: 13.8 us -> 0.66 us
  other arithmetic: 9.91 us -> 0 us
    reduce_scatter x1 -> x0, waiting for transfers between devices: 167 us -> none  [per_device(): lax.psum_scatter(lax.dot_general(grad_pre, w_in, (((0,), (0,)), ((), ()))...]
    all_gather x2 -> x0, waiting for transfers between devices: 133 us -> none  [the longest x1 74 us: per_device(): lax.all_gather(grad_z, 'dp', axis=0, tiled=True)]
    pallas_call x0 -> x1, Pallas kernels: none -> 122 us  [per_device(): pl.pallas_call(kernel, out_shape=[jax.ShapeDtypeStruct(shape, F32) for sh...]
    psum x1 -> x0, blocking collectives: 63.3 us -> none  [per_device(): in_total, out_total = lax.psum((in_part, out_part), 'dp')]
    dot_general x4 -> x0, matrix products: 43 us -> none  [the longest x1 12.2 us: per_device(): lax.dot_general(w_out, z_all, (((1,), (1,)), ((), ())), preferred_element...]
    psum x1 -> x0, waiting for transfers between devices: 40.6 us -> none  [per_device(): grad_wi, grad_wo = lax.psum((grad_wi, grad_wo), 'member')]
  transfers between devices with their start and end apart: 4 -> 0, of which waited for: 4 -> 0; matrix products, arithmetic and copies ran while one was open for 3% -> 0% of each run, Pallas kernels for 0% -> 0%
where the time goes in v1:
time: 132 us; the launch traced here: 131 us
  Pallas kernels  122 us (92%)
  local copies, waits for them, and re-layouts  8.23 us (6%)
    pallas_call x1, Pallas kernels, per_device(): pl.pallas_call(kernel, out_shape=[jax.ShapeDtypeStruct(shape, F32) for sh...  122 us
    unnamed x17, local copies, waits for them, and re-layouts  8.23 us

profile of v1, /device:TPU:16, one launch (start us, length us, event | category | flops | bytes accessed | tf_op | source)
XLA Modules:
  0.0 131.3 jit_solution(10423663458901000231)
XLA Ops:
  0.6 122.4 %shard_map.162 = (f32[128,896]{1,0:T(8,128)}, f32[480,896]{1,0:T(8,128)}, f32[480,896]{1,0:T(8,128)}, f32[1,896]{1,0:T(1,128)}, f32[1,480]{1,0:T(1,128)}, /*index=5*/f32[1,480]{1,0:T(1,128)}, f32[1,896]{1,0:T(1,128)}) custom-call(bf16[128,896]{1,0:T(8,128)(2,1)} %bitcast.7, bf16[128,896]{1,0:T(8,128)(2,1)} %bitcast.8, s32[1,128]{1,0:T(1,128)} %cnt_ref.1, ...), custom_call_target="tpu_custom_call" | custom-call | tf_op jit(solution)/shard_map/pallas_call | solution.py:422
  123.1 1.8 %copy.25 = f32[1,128,896]{2,1,0:T(8,128)} copy(f32[1,128,896]{2,1,0:T(8,128)} %bitcast.6) | data formatting | bytes 917504
  124.9 0.0 copy-start
  124.9 2.9 %copy.26 = f32[480,896]{1,0:T(8,128)} copy(f32[480,896]{1,0:T(8,128)} %get-tuple-element.29) | data formatting | bytes 3440640
  127.8 0.0 copy-done
  127.8 0.0 copy-start.2
  127.8 0.0 copy-start.4
  127.8 0.0 copy-start.3
  127.8 0.0 copy-start.1
  127.8 1.2 copy.27
  129.0 0.0 copy-done.2
  129.0 0.6 copy.28
  129.6 0.0 copy-done.4
  129.6 0.6 copy.29
  130.1 0.0 copy-done.3
  130.1 0.6 copy.30
  130.7 0.0 copy-done.1
  130.7 0.6 copy.31
Async XLA Ops:
  124.9 2.9 %copy-start = (f32[480,896]{1,0:T(8,128)S(1)}, f32[480,896]{1,0:T(8,128)}, u32[]{:S(2)}) copy-start(f32[480,896]{1,0:T(8,128)} %get-tuple-element.30) | copy-start | bytes 5160964
  127.8 1.2 copy-start.2
  127.8 1.8 %copy-start.4 = (f32[1,480]{1,0:T(1,128)S(1)}, f32[1,480]{1,0:T(1,128)}, u32[]{:S(2)}) copy-start(f32[1,480]{1,0:T(1,128)} %get-tuple-element.32) | copy-start | bytes 5764
  127.8 2.4 %copy-start.3 = (f32[1,480]{1,0:T(1,128)S(1)}, f32[1,480]{1,0:T(1,128)}, u32[]{:S(2)}) copy-start(f32[1,480]{1,0:T(1,128)} %get-tuple-element.33) | copy-start | bytes 5764
  127.8 3.0 %copy-start.1 = (f32[1,896]{1,0:T(1,128)S(1)}, f32[1,896]{1,0:T(1,128)}, u32[]{:S(2)}) copy-start(f32[1,896]{1,0:T(1,128)} %get-tuple-element.34) | copy-start | bytes 10756

commit v2 on v1

--- a/solution.py
+++ b/solution.py
@@ -16,7 +16,9 @@
 D = 896
 FB = 480
 NF = 2 * FB
-NH = 2
+PARTS = (4, 2, 2, 4)
+CA = 512
+WSCALE = 32768.0**-0.5
 
 HOPS = (
     (0, (0, 0), (7, 0)), (1, (0, 0), (1, 0)), (2, (0, 0), (0, 1)),
@@ -30,8 +32,8 @@
 
 def kernel(
     x_ref, dy_ref, cnt_ref, ph_ref, po_ref, wi_ref, wo_ref, ri_ref, si_ref, ro_ref, so_ref,
-    gx_ref, gwi_ref, gwo_ref, gri_ref, gsi_ref, gro_ref, gso_ref,
-    pre, slope, hid, gp, z_all, in_all, wo, wi, wt, rbuf, sbuf, acc_ro, acc_si, acc_in,
+    gx_ref, gw_ref, gri_ref, gsi_ref, gro_ref, gso_ref,
+    gwi_ref, gwo_ref, pre, slope, hid, gp, z_all, in_all, wo, wi, wt, rbuf, sbuf, acc_ro, acc_si, acc_in,
     col_s, col_r, part, sib_out, sib_in, mem_out, mem_x, mem_h, mem_all, vec_out, vec_in, vec_z,
     ring_s, ring_r, pre_l, pre_s, pre_r, w_l, w_s, w_r, col_ss, col_sr, acc_ss, acc_sr,
     sib_ss, sib_sr, x_s, x_r, h_s, h_r, all_s, all_r, vec_ss, vec_sr, vz_s, vz_r,
@@ -86,27 +88,30 @@
 
     pl.semaphore_wait(barrier, 8)
 
-    TP = TB // NH
-
-    def gather_send(u, buf, step, h):
+    Z, A, B, R = range(4)
+    columns = (pl.ds(0, D), pl.ds(0, CA), pl.ds(CA, D - CA))
+
+    def block(u, at, p):
+        rows = TB // PARTS[u]
+        return (z_all if u == Z else in_all).at[at[0], pl.ds(at[1] * TB + p * rows, rows), columns[u]]
+
+    def gather_send(u, step, p):
         for k in range(3 * step, 3 * step + 3):
-            way, (ss, sr), (ds, dr) = HOPS[k]
-            send(
-                buf.at[ss, pl.ds(sr * TB + h * TP, TP)], buf.at[ds, pl.ds(dr * TB + h * TP, TP)],
-                ring_s.at[u, k, h], ring_r.at[u, k, h], (zp, zm, yo)[way],
-            )
-
-    def gather_wait(u, buf, step, h):
+            way, src, dst = HOPS[k]
+            send(block(u, src, p), block(u, dst, p), ring_s.at[u, k, p], ring_r.at[u, k, p], (zp, zm, yo)[way])
+
+    def arrived(u, k, p, ref):
+        pltpu.make_async_remote_copy(
+            src_ref=ref, dst_ref=ref, send_sem=ring_s.at[u, k, p], recv_sem=ring_r.at[u, k, p],
+            device_id=yo, device_id_type=MESH,
+        ).wait_recv()
+
+    def gather_wait(u, step, p):
         for k in range(3 * step, 3 * step + 3):
-            way, _, (ds, dr) = HOPS[k]
-            part_ref = buf.at[ds, pl.ds(dr * TB + h * TP, TP)]
-            pltpu.make_async_remote_copy(
-                src_ref=part_ref, dst_ref=part_ref, send_sem=ring_s.at[u, k, h], recv_sem=ring_r.at[u, k, h],
-                device_id=(zp, zm, yo)[way], device_id_type=MESH,
-            ).wait_recv()
-
-    for h in range(NH):
-        gather_send(0, z_all, 0, h)
+            arrived(u, k, p, block(u, HOPS[k][2], p))
+
+    for p in range(PARTS[Z]):
+        gather_send(Z, 0, p)
 
     pre_in = {}
     for s in ORDER:
@@ -160,9 +165,9 @@
 
     UT = 240
 
-    def grad_pre(s):
+    def grad_pre(s, side):
         def tile(i, _):
-            rows = pl.ds(pl.multiple_of(i * UT, 16), UT)
+            rows = pl.ds(pl.multiple_of(side * FB + i * UT, 16), UT)
             u = lax.dot_general(wo[rows], z_all[s], (((1,), (1,)), ((), ())), preferred_element_type=F32)
             sc = col_s[rows]
             q = u * hid[s, rows].astype(F32)
@@ -174,7 +179,7 @@
             gp[s, rows, pl.ds(128, 128)] = (a[:, 128:] * sc).astype(BF)
             return 0
 
-        lax.fori_loop(0, NF // UT, tile, 0)
+        lax.fori_loop(0, FB // UT, tile, 0)
 
     HT = 448
 
@@ -188,69 +193,83 @@
 
     WT = 240
 
-    def grad_w(out, lhs, rhs, side, slots, first):
+    def grad_w(g, side, slots, first):
+        lhs, rhs = (hid, z_all) if g == 0 else (gp, in_all)
+        out, cols = (part if side else accs[g]), columns[g]
+
         def tile(i, _):
             rows = pl.ds(pl.multiple_of(i * WT, 16), WT)
             src = pl.ds(pl.multiple_of(side * FB + i * WT, 16), WT)
             for n, s in enumerate(slots):
-                t = jnp.dot(lhs[s, src], rhs[s], preferred_element_type=F32)
+                t = jnp.dot(lhs[s, src], rhs[s, :, cols], preferred_element_type=F32)
                 if first and n == 0:
-                    out[rows] = t
+                    out[rows, cols] = t
                 else:
-                    out[rows] += t
+                    out[rows, cols] += t
             return 0
 
         lax.fori_loop(0, FB // WT, tile, 0)
 
-    outs = (gwo_ref, gwi_ref)
+    accs = (gwo_ref, gwi_ref, gwi_ref)
+    which = (0, 1, 1)
     stage = {}
 
     def piece(xx):
         return pl.ds(pl.multiple_of(112 * xx + 16 * (xx // 2), 16), 128)
 
     def w_sib(g):
-        sib_out[g] = part[...].astype(BF)
-        stage["sib", g] = send(sib_out.at[g], sib_in.at[g], sib_ss.at[g], sib_sr.at[g], co)
+        a, cols = which[g], columns[g]
+        sib_out[a, :, cols] = part[:, cols].astype(BF)
+        stage["sib", g] = send(sib_out.at[a, :, cols], sib_in.at[a, :, cols], sib_ss.at[g], sib_sr.at[g], co)
 
     def w_x(g):
+        a, cols = which[g], columns[g]
         stage["sib", g].wait_recv()
-        outs[g][...] += sib_in[g].astype(F32)
-        mem_out[g] = outs[g][...].astype(BF)
+        t = accs[g][:, cols] + sib_in[a, :, cols].astype(F32)
+        accs[g][:, cols] = t
+        mem_out[a, :, cols] = t.astype(BF)
         stage["x", g] = [
-            send(mem_out.at[g, piece(lax.rem(x + k, 4))], mem_x.at[g, k - 1], x_s.at[g, k - 1], x_r.at[g, k - 1], xs[k - 1])
-            for k in (1, 2, 3)
+            send(
+                mem_out.at[a, piece(lax.rem(x + k, 4)), cols], mem_x.at[a, k - 1, :, cols],
+                x_s.at[g, k - 1], x_r.at[g, k - 1], xs[k - 1],
+            )
+            for k in (2, 1, 3)
         ]
 
     def w_h(g):
+        a, cols = which[g], columns[g]
         for copy in stage["x", g]:
             copy.wait_recv()
-        total = outs[g][piece(x)]
+        total = accs[g][piece(x), cols]
         for k in range(3):
-            total += mem_x[g, k].astype(F32)
-        mem_h[g, 0] = total.astype(BF)
-        stage["h", g] = send(mem_h.at[g, 0], mem_h.at[g, 1], h_s.at[g], h_r.at[g], ho)
+            total += mem_x[a, k, :, cols].astype(F32)
+        mem_h[a, 0, :, cols] = total.astype(BF)
+        stage["h", g] = send(mem_h.at[a, 0, :, cols], mem_h.at[a, 1, :, cols], h_s.at[g], h_r.at[g], ho)
 
     def w_all(g):
+        a, cols = which[g], columns[g]
         stage["h", g].wait_recv()
-        mem_all[g, 0] = (mem_h[g, 0].astype(F32) + mem_h[g, 1].astype(F32)).astype(BF)
+        mem_all[a, 0, :, cols] = (mem_h[a, 0, :, cols].astype(F32) + mem_h[a, 1, :, cols].astype(F32)).astype(BF)
         stage["all", g] = [
-            send(mem_all.at[g, 0], mem_all.at[g, k], all_s.at[g, k - 1], all_r.at[g, k - 1], xs[k - 1])
-            for k in (1, 2, 3)
+            send(mem_all.at[a, 0, :, cols], mem_all.at[a, k, :, cols], all_s.at[g, k - 1], all_r.at[g, k - 1], xs[k - 1])
+            for k in (2, 1, 3)
         ]
 
     def w_end(g):
+        a, cols = which[g], columns[g]
         for copy in stage["all", g]:
             copy.wait_recv()
         for xx in range(4):
             rows = pl.ds(112 * xx + 16 * (xx // 2), 128)
-            outs[g][rows] = mem_all[g, lax.rem(x + 4 - xx, 4)].astype(F32) * (32768.0**-0.5)
-
-    def v_part(side, grads):
-        t = jnp.sum(wi[pl.ds(side * FB, FB)].astype(F32) * grads[...], axis=0, keepdims=True)
+            gw_ref[a, rows, cols] = mem_all[a, lax.rem(x + 4 - xx, 4), :, cols]
+
+    def v_part(g, side):
+        cols, grads = columns[g], part if side else accs[g]
+        t = jnp.sum(wi[pl.ds(side * FB, FB), cols].astype(F32) * grads[:, cols], axis=0, keepdims=True)
         if side == 1:
-            vec_out[0, pl.ds(1, 1)] = t
+            vec_out[0, pl.ds(1, 1), cols] = t
         else:
-            vec_out[0, pl.ds(1, 1)] += t
+            vec_out[0, pl.ds(1, 1), cols] += t
 
     def v_pair(i, dev):
         stage["v", i] = send(vec_out.at[i], vec_in.at[i], vec_ss.at[i], vec_sr.at[i], dev)
@@ -305,10 +324,10 @@
         w_in[0].wait_recv()
         w_copies[0].wait()
 
-    DP = D // NH
-
-    def sum_send(step, h):
-        rows = pl.ds(h * DP, DP)
+    DP = D // PARTS[R]
+
+    def sum_send(step, p):
+        rows = pl.ds(p * DP, DP)
         for k in range(3 * step, 3 * step + 3):
             way, _, (ds, dr) = HOPS[k]
             t = slope[ds, rows, pl.ds(dr * TB, TB)]
@@ -316,102 +335,88 @@
                 if HOPS[k2][1] == (ds, dr):
                     t += rbuf[k2, rows].astype(F32)
             sbuf[k, rows] = t.astype(BF)
-            send(
-                sbuf.at[k, rows], rbuf.at[k, rows], ring_s.at[2, k, h], ring_r.at[2, k, h], (zm, zp, yo)[way]
-            )
-
-    def sum_wait(step, h):
+            send(sbuf.at[k, rows], rbuf.at[k, rows], ring_s.at[R, k, p], ring_r.at[R, k, p], (zm, zp, yo)[way])
+
+    def sum_wait(step, p):
         for k in range(3 * step, 3 * step + 3):
-            way = HOPS[k][0]
-            ref = rbuf.at[k, pl.ds(h * DP, DP)]
-            pltpu.make_async_remote_copy(
-                src_ref=ref, dst_ref=ref, send_sem=ring_s.at[2, k, h], recv_sem=ring_r.at[2, k, h],
-                device_id=(zm, zp, yo)[way], device_id_type=MESH,
-            ).wait_recv()
+            arrived(R, k, p, rbuf.at[k, pl.ds(p * DP, DP)])
 
     def col_wait():
         for copy in col_in:
             copy.wait_recv()
 
-    def z_wait():
-        for h in range(NH):
-            gather_wait(0, z_all, 4, h)
+    def gathered(u):
+        for p in range(PARTS[u]):
+            gather_wait(u, 4, p)
 
     f = functools.partial
-    z_work = [
-        [f(gelu, 0, 0), f(gelu, 7, 0)],
-        [col_wait, f(gelu, 0, 1)],
-        [wait_wo, f(gelu, 7, 1), f(gelu, 1, 0)],
-        [f(gelu, 1, 1), f(grad_pre, 0)],
-        [f(gelu, 2, 0), f(gelu, 2, 1)],
-        [f(gelu, 6, 0), f(grad_pre, 7)],
-        [f(gelu, 6, 1), f(gelu, 5, 0)],
-        [f(gelu, 5, 1), f(grad_pre, 1)],
-        [f(gelu, 3, 0), f(gelu, 3, 1)],
-        [f(gelu, 4, 0), f(gelu, 4, 1)],
-    ]
-    in_work = [
-        [f(grad_pre, 2), transpose_w],
-        [f(grad_pre, 6), f(grad_h, 6)],
-        [z_wait, f(grad_pre, 5), f(grad_h, 5)],
-        [f(grad_pre, 3), f(grad_h, 3)],
-        [f(grad_pre, 4), f(grad_h, 4), acc_send],
-        [f(grad_w, part, hid, z_all, 1, ORDER, True), f(w_sib, 0), f(grad_h, 2)],
-        [f(grad_w, gwo_ref, hid, z_all, 0, ORDER, True), f(grad_h, 7)],
-        [f(w_x, 0), f(grad_h, 1), f(grad_h, 0)],
-        [f(grad_w, part, gp, in_all, 1, ORDER[:3], True), acc_end],
-        [f(grad_w, gwi_ref, gp, in_all, 0, ORDER[:3], True), f(w_h, 0)],
-    ]
-    sum_work = [
-        [f(grad_w, part, gp, in_all, 1, ORDER[3:], False), f(w_sib, 1), f(v_part, 1, part)],
-        [f(grad_w, gwi_ref, gp, in_all, 0, ORDER[3:], False), f(v_part, 0, gwi_ref), f(v_pair, 0, co)],
-        [f(w_x, 1), f(w_all, 0), f(v_sum, 0), f(v_pair, 1, yo)],
-        [f(v_sum, 1), f(v_send, 0)],
-        [f(w_end, 0)],
-        [f(w_h, 1), f(v_wait, 0), f(v_send, 1)],
-        [f(v_wait, 1), f(v_send, 2)],
-        [f(v_wait, 2), f(v_send, 3)],
-        [f(w_all, 1)],
-        [f(v_wait, 3), v_end],
-    ]
-
-    for step in range(5):
-        for h in range(NH):
-            if step:
-                gather_wait(0, z_all, step - 1, h)
-                gather_send(0, z_all, step, h)
-            for job in z_work[2 * step + h]:
+    early, late = ORDER[:5], ORDER[5:]
+    plan = (
+        (Z, 0, ((f(gelu, 0, 0),), (f(gelu, 7, 0),), (f(gelu, 1, 0),), (f(gelu, 2, 0),))),
+        (Z, 1, ((col_wait, f(gelu, 0, 1)), (f(gelu, 7, 1),), (f(gelu, 1, 1),), (wait_wo, f(grad_pre, 0, 0)))),
+        (Z, 2, ((f(grad_pre, 0, 1),), (f(gelu, 6, 0), f(gelu, 6, 1)), (f(gelu, 2, 1), f(gelu, 5, 0)), (f(grad_pre, 7, 0),))),
+        (A, 0, ((f(grad_pre, 7, 1),), (f(gelu, 5, 1), f(gelu, 3, 0)))),
+        (Z, 3, ((f(gelu, 3, 1),), (f(gelu, 4, 0),), (f(gelu, 4, 1),), (f(grad_pre, 1, 0),))),
+        (Z, 4, ((f(grad_pre, 1, 1),), (transpose_w,), (f(grad_h, 0),), (f(grad_pre, 2, 0),))),
+        (A, 1, ((f(grad_pre, 2, 1),), (f(grad_pre, 6, 0),))),
+        (B, 0, ((f(grad_pre, 6, 1),), (f(grad_h, 6),))),
+        (A, 2, ((f(gathered, Z), f(grad_w, 0, 1, ORDER[:4], True)), (f(grad_w, 0, 1, ORDER[4:], False), f(w_sib, 0)))),
+        (B, 1, ((f(grad_w, 0, 0, ORDER[:4], True),), (f(grad_w, 0, 0, ORDER[4:], False),))),
+        (A, 3, ((f(grad_pre, 5, 0),), (f(grad_pre, 5, 1),))),
+        (B, 2, ((f(w_x, 0), f(grad_pre, 3, 0)), (f(grad_pre, 3, 1),))),
+        (A, 4, ((f(grad_pre, 4, 0),), (f(grad_pre, 4, 1), acc_send))),
+        (B, 3, ((f(grad_h, 5), f(grad_h, 3)), (f(grad_h, 4), f(grad_h, 2)))),
+        (R, 4, (
+            (f(grad_w, 1, 1, early, True),), (f(grad_w, 1, 0, early, True),),
+            (f(gathered, A), f(grad_w, 1, 1, late, False), f(w_sib, 1)),
+            (f(grad_w, 1, 0, late, False), f(v_part, 1, 1), f(v_part, 1, 0)),
+        )),
+        (B, 4, ((f(w_x, 1), f(w_h, 0)), (f(grad_w, 2, 1, early, True),))),
+        (R, 3, (
+            (f(grad_w, 2, 0, early, True),), (f(grad_h, 1),),
+            (f(gathered, B), f(grad_w, 2, 1, late, False), f(w_sib, 2)),
+            (f(grad_w, 2, 0, late, False), f(v_part, 2, 1), f(v_part, 2, 0)),
+        )),
+        (R, 2, ((f(w_x, 2), f(v_pair, 0, co)), (f(grad_h, 7), acc_end), (f(w_all, 0), f(v_sum, 0), f(v_pair, 1, yo)), ())),
+        (R, 1, ((f(w_h, 1), f(v_sum, 1), f(v_send, 0)), (), (f(v_wait, 0), f(v_send, 1)), (f(w_h, 2),))),
+        (R, 0, ((f(w_all, 1), f(v_wait, 1), f(v_send, 2)), (f(w_end, 0),), (f(w_all, 2), f(v_wait, 2), f(v_send, 3)), ())),
+    )
+    for n, (u, step, work) in enumerate(plan):
+        for p in range(PARTS[u]):
+            if u == R:
+                if step < 4:
+                    sum_wait(step + 1, p)
+                sum_send(step, p)
+            elif n:
+                if step:
+                    gather_wait(u, step - 1, p)
+                gather_send(u, step, p)
+            for job in work[p]:
                 job()
-    for h in range(NH):
-        gather_send(1, in_all, 0, h)
-    for step in range(5):
-        for h in range(NH):
-            if step:
-                gather_wait(1, in_all, step - 1, h)
-                gather_send(1, in_all, step, h)
-            for job in in_work[2 * step + h]:
-                job()
-    for step in range(5):
-        for h in range(NH):
-            if step:
-                sum_wait(5 - step, h)
-            sum_send(4 - step, h)
-            if step == 0 and h == 0:
-                for hh in range(NH):
-                    gather_wait(1, in_all, 4, hh)
-            for job in sum_work[2 * step + h]:
-                job()
-    for h in range(NH):
-        sum_wait(0, h)
+    w_end(1)
+    v_wait(3)
+    v_end()
+    for p in range(PARTS[R]):
+        sum_wait(0, p)
     for j in range(D // 128):
         cs = pl.ds(j * 128, 128)
         t = slope[0, cs, pl.ds(0, TB)]
         for k in range(3):
             t += rbuf[k, cs].astype(F32)
         gx_ref[:, cs] = t.T * ri_ref[:, cs]
-    w_end(1)
+    w_end(2)
     for copy in sent:
         copy.wait_send()
+
+
+def finish(gx, gw, gri, gsi, gro, gso, gx_out, gwi_out, gwo_out, gri_out, gsi_out, gro_out, gso_out):
+    gwo_out[...] = gw[0].astype(F32) * WSCALE
+    gwi_out[...] = gw[1].astype(F32) * WSCALE
+
+    @pl.when(pl.program_id(0) == 0)
+    def _():
+        for src, dst in ((gx, gx_out), (gri, gri_out), (gsi, gsi_out), (gro, gro_out), (gso, gso_out)):
+            dst[...] = src[...]
 
 
 def per_device(
@@ -419,15 +424,15 @@
 ):
     vm, hbm = pl.BlockSpec(memory_space=pltpu.VMEM), pl.BlockSpec(memory_space=pl.ANY)
     dma = pltpu.SemaphoreType.DMA
+    shapes = (((TB, D), F32), ((2, FB, D), BF), ((1, D), F32), ((1, FB), F32), ((1, FB), F32), ((1, D), F32))
     outs = pl.pallas_call(
         kernel,
-        out_shape=[
-            jax.ShapeDtypeStruct(shape, F32)
-            for shape in ((TB, D), (FB, D), (FB, D), (1, D), (1, FB), (1, FB), (1, D))
-        ],
+        out_shape=[jax.ShapeDtypeStruct(shape, dtype) for shape, dtype in shapes],
         in_specs=[vm, vm, vm, hbm, vm, hbm, hbm, vm, vm, vm, vm],
-        out_specs=[vm] * 7,
+        out_specs=[vm] * 6,
         scratch_shapes=[
+            pltpu.VMEM((FB, D), F32),
+            pltpu.VMEM((FB, D), F32),
             pltpu.VMEM((NZ, NF, 2 * TB), BF),
             pltpu.VMEM((NZ, NF, 2 * TB), F32),
             pltpu.VMEM((NZ, NF, 2 * TB), BF),
@@ -454,15 +459,15 @@
             pltpu.VMEM((2, 8, D), F32),
             pltpu.VMEM((2, 8, D), F32),
             pltpu.VMEM((NZ, 8, D), F32),
-            dma((3, 15, NH)), dma((3, 15, NH)),
+            dma((4, 15, 4)), dma((4, 15, 4)),
             dma((NZ, 2)), dma((NZ, 2)), dma((NZ, 2)),
             dma((2,)), dma((2,)), dma((2,)),
             dma((2,)), dma((2,)),
             dma((2,)), dma((2,)),
-            dma((2,)), dma((2,)),
-            dma((2, 3)), dma((2, 3)),
-            dma((2,)), dma((2,)),
-            dma((2, 3)), dma((2, 3)),
+            dma((3,)), dma((3,)),
+            dma((3, 3)), dma((3, 3)),
+            dma((3,)), dma((3,)),
+            dma((3, 3)), dma((3, 3)),
             dma((2,)), dma((2,)),
             dma((2, 4)), dma((2, 4)),
         ],
@@ -470,7 +475,24 @@
             collective_id=0, has_side_effects=True, vmem_limit_bytes=63 * 2**20
         ),
     )(inputs[0], cotangent[0], counts, pre_hidden[0], pre_out[0], w_in, w_out, r_in, s_in, r_out, s_out)
-    gx, gwi, gwo, gri, gsi, gro, gso = outs
+    steps = 3
+
+    def whole(shape):
+        return pl.BlockSpec(shape, lambda i: (0,) * len(shape))
+
+    rows = pl.BlockSpec((FB // steps, D), lambda i: (i, 0))
+    small = [whole(shape) for shape, _ in shapes[2:]]
+    gx, gwi, gwo, gri, gsi, gro, gso = pl.pallas_call(
+        finish,
+        grid=(steps,),
+        out_shape=[
+            jax.ShapeDtypeStruct(shape, F32)
+            for shape in ((TB, D), (FB, D), (FB, D), (1, D), (1, FB), (1, FB), (1, D))
+        ],
+        in_specs=[whole((TB, D)), pl.BlockSpec((2, FB // steps, D), lambda i: (0, i, 0)), *small],
+        out_specs=[whole((TB, D)), rows, rows, *small],
+        compiler_params=pltpu.CompilerParams(vmem_limit_bytes=63 * 2**20),
+    )(*outs)
     return gx[None], gwi, gwo, gri, gsi, gro, gso
 
 

time: 132 us -> 113 us (0.86); the launches traced: 131 us -> 111 us
  Pallas kernels: 122 us -> 110 us
  local copies, waits for them, and re-layouts: 8.23 us -> 0 us
    pallas_call x1 -> x2, Pallas kernels: 122 us -> 110 us  [the longest x1 106 us: per_device(): pl.pallas_call(kernel, out_shape=[jax.ShapeDtypeStruct(shape, dtype) for...]
    unnamed x17 -> x0, local copies, waits for them, and re-layouts: 8.23 us -> none
where the time goes in v2:
time: 113 us; the launch traced here: 111 us
  Pallas kernels  110 us (97%)
    pallas_call x1, Pallas kernels, per_device(): pl.pallas_call(kernel, out_shape=[jax.ShapeDtypeStruct(shape, dtype) for...  106 us
    pallas_call x1, Pallas kernels, per_device(): pl.pallas_call(finish, grid=(steps,), out_shape=[jax.ShapeDtypeStruct(sha...  4.16 us

profile of v2, /device:TPU:16, one launch (start us, length us, event | category | flops | bytes accessed | tf_op | source)
XLA Modules:
  0.0 110.8 jit_solution(11677726351414987623)
XLA Ops:
  0.6 105.9 %shard_map.162 = (f32[128,896]{1,0:T(8,128)}, bf16[2,480,896]{2,1,0:T(8,128)(2,1)}, f32[1,896]{1,0:T(1,128)}, f32[1,480]{1,0:T(1,128)}, f32[1,480]{1,0:T(1,128)}, /*index=5*/f32[1,896]{1,0:T(1,128)}) custom-call(bf16[128,896]{1,0:T(8,128)(2,1)} %bitcast.6, bf16[128,896]{1,0:T(8,128)(2,1)} %bitcast.7, s32[1,128]{1,0:T(1,128)} %cnt_ref.1, ...), custom_call_target="tpu_custom_call" | custom-call | tf_op jit(solution)/shard_map/pallas_call | solution.py:428
  106.5 4.2 %shard_map.163 = (f32[128,896]{1,0:T(8,128)}, f32[480,896]{1,0:T(8,128)}, f32[480,896]{1,0:T(8,128)}, f32[1,896]{1,0:T(1,128)}, f32[1,480]{1,0:T(1,128)}, /*index=5*/f32[1,480]{1,0:T(1,128)}, f32[1,896]{1,0:T(1,128)}) custom-call(f32[128,896]{1,0:T(8,128)} %get-tuple-element.20.gx, bf16[2,480,896]{2,1,0:T(8,128)(2,1)} %get-tuple-element.21.gw, ...), custom_call_target="tpu_custom_call" | custom-call | tf_op jit(solution)/shard_map/pallas_call | solution.py:485

commit v3 on v2

--- a/solution.py
+++ b/solution.py
@@ -27,13 +27,16 @@
     (0, (5, 0), (4, 0)), (1, (1, 1), (2, 1)), (2, (6, 0), (6, 1)),
     (0, (6, 1), (5, 1)), (1, (2, 1), (3, 1)), (2, (4, 0), (4, 1)),
 )
+LAST = ((0, (5, 1), (4, 1)), (0, (5, 1), (4, 1)), (1, (3, 1), (4, 1)), (1, (3, 1), (4, 1)))
+SUM_STEPS = ((0, 1, 2), (3, 4), (6, 7, 8), (9, 10, 11), (12, 13), (14, 5))
+SUM_ROWS = ((0, 256), (256, 256), (512, 256), (768, 128))
 ORDER = (0, 7, 1, 2, 6, 5, 3, 4)
 
 
 def kernel(
-    x_ref, dy_ref, cnt_ref, ph_ref, po_ref, wi_ref, wo_ref, ri_ref, si_ref, ro_ref, so_ref,
+    x_hbm, dy_hbm, cnt_ref, ph_ref, po_hbm, wi_ref, wo_ref, ri_ref, si_ref, ro_ref, so_ref,
     gx_ref, gw_ref, gri_ref, gsi_ref, gro_ref, gso_ref,
-    gwi_ref, gwo_ref, pre, slope, hid, gp, z_all, in_all, wo, wi, wt, rbuf, sbuf, acc_ro, acc_si, acc_in,
+    x_ref, dy_ref, po_ref, own_l, gwi_ref, gwo_ref, pre, slope, hid, gp, z_all, in_all, wo, wi, wt, rbuf, sbuf, acc_ro, acc_si, acc_in,
     col_s, col_r, part, sib_out, sib_in, mem_out, mem_x, mem_h, mem_all, vec_out, vec_in, vec_z,
     ring_s, ring_r, pre_l, pre_s, pre_r, w_l, w_s, w_r, col_ss, col_sr, acc_ss, acc_sr,
     sib_ss, sib_sr, x_s, x_r, h_s, h_r, all_s, all_r, vec_ss, vec_sr, vz_s, vz_r,
@@ -47,6 +50,7 @@
     co = (m, z * 4 + y * 2 + (1 - c))
     xs = [(yh * 4 + lax.rem(x + k, 4), d) for k in (1, 2, 3)]
     ho = ((1 - yh) * 4 + x, d)
+    zs_all = [(m, lax.rem(z + k, NZ) * 4 + y * 2 + c) for k in range(1, NZ)]
     sent = []
 
     def send(src, dst, ss, rs, dev):
@@ -58,20 +62,15 @@
         return copy
 
     barrier = pltpu.get_barrier_semaphore()
-    for dev in (zp, zm, yo, co, ho, *xs):
+    for dev in (yo, co, ho, *xs, *zs_all):
         pl.semaphore_signal(barrier, inc=1, device_id=dev, device_id_type=MESH)
 
-    local = []
-    for i, s in enumerate(ORDER):
-        zs = lax.rem(z + s, NZ)
-        for r in range(2):
-            yy = y if r == 0 else 1 - y
-            col = pl.multiple_of((zs * 4 + yy * 2 + c) * TB, TB)
-            copy = pltpu.make_async_copy(
-                ph_ref.at[:, pl.ds(col, TB)], pre.at[s, pl.ds(0, FB), pl.ds(r * TB, TB)], pre_l.at[s, r]
-            )
-            copy.start()
-            local.append(copy)
+    own = [
+        pltpu.make_async_copy(src, dst, own_l.at[i])
+        for i, (src, dst) in enumerate(((dy_hbm, dy_ref), (x_hbm, x_ref), (po_hbm, po_ref)))
+    ]
+    for copy in own:
+        copy.start()
     w_copies = []
     for i, (src, dst) in enumerate(((wo_ref, wo), (wi_ref, wi))):
         copy = pltpu.make_async_copy(src, dst.at[pl.ds(0, FB)], w_l.at[i])
@@ -79,14 +78,12 @@
         w_copies.append(copy)
 
     cnt = jnp.broadcast_to(cnt_ref[...].astype(F32), (TB, TB)).T
+    own[0].wait()
     for j in range(D // 128):
         cs = pl.ds(j * 128, 128)
-        weighted = dy_ref[:, cs].astype(F32) * cnt
-        z_all[0, pl.ds(0, TB), cs] = (weighted * so_ref[:, cs]).astype(BF)
-        in_all[0, pl.ds(0, TB), cs] = (x_ref[:, cs].astype(F32) * ri_ref[:, cs]).astype(BF)
-        vec_out[0, pl.ds(0, 1), cs] = jnp.sum(weighted * po_ref[:, cs].astype(F32), axis=0, keepdims=True)
-
-    pl.semaphore_wait(barrier, 8)
+        z_all[0, pl.ds(0, TB), cs] = (dy_ref[:, cs].astype(F32) * cnt * so_ref[:, cs]).astype(BF)
+
+    pl.semaphore_wait(barrier, 13)
 
     Z, A, B, R = range(4)
     columns = (pl.ds(0, D), pl.ds(0, CA), pl.ds(CA, D - CA))
@@ -98,44 +95,74 @@
     def gather_send(u, step, p):
         for k in range(3 * step, 3 * step + 3):
             way, src, dst = HOPS[k]
+            for k2 in range(15):
+                if HOPS[k2][2] == src:
+                    need(u, k2, p)
             send(block(u, src, p), block(u, dst, p), ring_s.at[u, k, p], ring_r.at[u, k, p], (zp, zm, yo)[way])
 
-    def arrived(u, k, p, ref):
+    done = set()
+
+    def need(u, k, p):
+        if (u, k, p) in done:
+            return
+        done.add((u, k, p))
+        ref = rbuf.at[k, pl.ds(*SUM_ROWS[p])] if u == R else block(u, HOPS[k][2], p)
         pltpu.make_async_remote_copy(
             src_ref=ref, dst_ref=ref, send_sem=ring_s.at[u, k, p], recv_sem=ring_r.at[u, k, p],
             device_id=yo, device_id_type=MESH,
         ).wait_recv()
 
-    def gather_wait(u, step, p):
-        for k in range(3 * step, 3 * step + 3):
-            arrived(u, k, p, block(u, HOPS[k][2], p))
+    def need_slots(u, slots):
+        for k, hop in enumerate(HOPS):
+            if hop[2][0] in slots:
+                for p in range(PARTS[u]):
+                    need(u, k, p)
 
     for p in range(PARTS[Z]):
         gather_send(Z, 0, p)
-
-    pre_in = {}
+    own[1].wait()
+    own[2].wait()
+    for j in range(D // 128):
+        cs = pl.ds(j * 128, 128)
+        weighted = dy_ref[:, cs].astype(F32) * cnt
+        in_all[0, pl.ds(0, TB), cs] = (x_ref[:, cs].astype(F32) * ri_ref[:, cs]).astype(BF)
+        vec_out[0, pl.ds(j, 1)] = jnp.sum(weighted * po_ref[:, cs].astype(F32), axis=0, keepdims=True)
+
+    def patches(s, r, core):
+        zs = lax.rem(z + s, NZ)
+        yy = y if r == 0 else 1 - y
+        return ph_ref.at[:, pl.ds(pl.multiple_of((zs * 4 + yy * 2 + core) * TB, TB), TB)]
+
+    local, pre_in = {}, {}
     for s in ORDER:
-        zs = lax.rem(z + s, NZ)
         for r in range(2):
-            yy = y if r == 0 else 1 - y
-            col = pl.multiple_of((zs * 4 + yy * 2 + (1 - c)) * TB, TB)
+            local[s, r] = pltpu.make_async_copy(
+                patches(s, r, c), pre.at[s, pl.ds(0, FB), pl.ds(r * TB, TB)], pre_l.at[s, r]
+            )
+            local[s, r].start()
+
+    def pre_send(s):
+        for r in range(2):
             pre_in[s, r] = send(
-                ph_ref.at[:, pl.ds(col, TB)], pre.at[s, pl.ds(FB, FB), pl.ds(r * TB, TB)],
+                patches(s, r, 1 - c), pre.at[s, pl.ds(FB, FB), pl.ds(r * TB, TB)],
                 pre_s.at[s, r], pre_r.at[s, r], co,
             )
-        if s == 0:
-            col_s[pl.ds(0, FB)] = jnp.broadcast_to(si_ref[...], (128, FB)).T
-            col_r[pl.ds(0, FB)] = jnp.broadcast_to(ro_ref[...], (128, FB)).T
-            col_in = [
-                send(b.at[pl.ds(0, FB)], b.at[pl.ds(FB, FB)], col_ss.at[i], col_sr.at[i], co)
-                for i, b in enumerate((col_s, col_r))
-            ]
-        if s == 7:
-            w_in = [
-                send(src, dst.at[pl.ds(FB, FB)], w_s.at[i], w_r.at[i], co)
-                for i, (src, dst) in enumerate(((wo_ref, wo), (wi_ref, wi)))
-            ]
-    vec_out[0, pl.ds(2, 6)] = jnp.zeros((6, D), F32)
+
+    w_in = {}
+
+    def w_send(i):
+        src, dst = ((wo_ref, wo), (wi_ref, wi))[i]
+        w_in[i] = send(src, dst.at[pl.ds(FB, FB)], w_s.at[i], w_r.at[i], co)
+
+    pre_send(0)
+    col_s[pl.ds(0, FB)] = jnp.broadcast_to(si_ref[...], (128, FB)).T
+    col_r[pl.ds(0, FB)] = jnp.broadcast_to(ro_ref[...], (128, FB)).T
+    col_in = [
+        send(b.at[pl.ds(0, FB)], b.at[pl.ds(FB, FB)], col_ss.at[i], col_sr.at[i], co)
+        for i, b in enumerate((col_s, col_r))
+    ]
+    vec_out[0, pl.ds(7, 1)] = jnp.zeros((1, 128), F32)
+    vec_out[0, pl.ds(15, 1)] = jnp.zeros((1, 128), F32)
     acc_ro[...] = jnp.zeros_like(acc_ro)
     acc_si[...] = jnp.zeros_like(acc_si)
 
@@ -144,7 +171,7 @@
     def gelu(s, side):
         if side == 0:
             for r in range(2):
-                local[2 * ORDER.index(s) + r].wait()
+                local[s, r].wait()
         else:
             for r in range(2):
                 pre_in[s, r].wait_recv()
@@ -166,6 +193,8 @@
     UT = 240
 
     def grad_pre(s, side):
+        need_slots(Z, (s,))
+
         def tile(i, _):
             rows = pl.ds(pl.multiple_of(side * FB + i * UT, 16), UT)
             u = lax.dot_general(wo[rows], z_all[s], (((1,), (1,)), ((), ())), preferred_element_type=F32)
@@ -196,6 +225,7 @@
     def grad_w(g, side, slots, first):
         lhs, rhs = (hid, z_all) if g == 0 else (gp, in_all)
         out, cols = (part if side else accs[g]), columns[g]
+        need_slots(g, slots)
 
         def tile(i, _):
             rows = pl.ds(pl.multiple_of(i * WT, 16), WT)
@@ -264,12 +294,14 @@
             gw_ref[a, rows, cols] = mem_all[a, lax.rem(x + 4 - xx, 4), :, cols]
 
     def v_part(g, side):
-        cols, grads = columns[g], part if side else accs[g]
-        t = jnp.sum(wi[pl.ds(side * FB, FB), cols].astype(F32) * grads[:, cols], axis=0, keepdims=True)
-        if side == 1:
-            vec_out[0, pl.ds(1, 1), cols] = t
-        else:
-            vec_out[0, pl.ds(1, 1), cols] += t
+        grads = part if side else accs[g]
+        for j in range(CA // 128) if g == 1 else range(CA // 128, D // 128):
+            cs = pl.ds(j * 128, 128)
+            t = jnp.sum(wi[pl.ds(side * FB, FB), cs].astype(F32) * grads[:, cs], axis=0, keepdims=True)
+            if side == 1:
+                vec_out[0, pl.ds(8 + j, 1)] = t
+            else:
+                vec_out[0, pl.ds(8 + j, 1)] += t
 
     def v_pair(i, dev):
         stage["v", i] = send(vec_out.at[i], vec_in.at[i], vec_ss.at[i], vec_sr.at[i], dev)
@@ -282,22 +314,21 @@
         else:
             vec_z[0] = t
 
-    def v_send(k):
-        stage["va", k] = send(vec_z.at[(8 - k) % 8], vec_z.at[7 - k], vz_s.at[0, k], vz_r.at[0, k], zp)
-        if k < 3:
-            stage["vb", k] = send(vec_z.at[k], vec_z.at[k + 1], vz_s.at[1, k], vz_r.at[1, k], zm)
-
-    def v_wait(k):
-        stage["va", k].wait_recv()
-        if k < 3:
-            stage["vb", k].wait_recv()
+    def v_send():
+        stage["vz"] = [
+            send(vec_z.at[0], vec_z.at[NZ - k], vz_s.at[k - 1], vz_r.at[k - 1], zs_all[k - 1]) for k in range(1, NZ)
+        ]
 
     def v_end():
+        for copy in stage["vz"]:
+            copy.wait_recv()
         total = vec_z[lax.rem(NZ - z, NZ)]
         for s in range(1, NZ):
             total += vec_z[lax.rem(s + NZ - z, NZ)]
-        gso_ref[...] = total[0:1] * (1.0 / 64.0)
-        gri_ref[...] = total[1:2] / ri_ref[...] * (1.0 / 64.0)
+        for j in range(D // 128):
+            cs = pl.ds(j * 128, 128)
+            gso_ref[:, cs] = total[j:j + 1] * (1.0 / 64.0)
+            gri_ref[:, cs] = total[8 + j:9 + j] / ri_ref[:, cs] * (1.0 / 64.0)
 
     def acc_send():
         stage["acc"] = [
@@ -324,98 +355,126 @@
         w_in[0].wait_recv()
         w_copies[0].wait()
 
-    DP = D // PARTS[R]
-
     def sum_send(step, p):
-        rows = pl.ds(p * DP, DP)
-        for k in range(3 * step, 3 * step + 3):
-            way, _, (ds, dr) = HOPS[k]
+        rows = pl.ds(*SUM_ROWS[p])
+        hops = (*HOPS[:14], LAST[p])
+        for k in SUM_STEPS[step]:
+            way, _, (ds, dr) = hops[k]
             t = slope[ds, rows, pl.ds(dr * TB, TB)]
             for k2 in range(15):
-                if HOPS[k2][1] == (ds, dr):
+                if hops[k2][1] == (ds, dr):
+                    need(R, k2, p)
                     t += rbuf[k2, rows].astype(F32)
             sbuf[k, rows] = t.astype(BF)
             send(sbuf.at[k, rows], rbuf.at[k, rows], ring_s.at[R, k, p], ring_r.at[R, k, p], (zm, zp, yo)[way])
 
-    def sum_wait(step, p):
-        for k in range(3 * step, 3 * step + 3):
-            arrived(R, k, p, rbuf.at[k, pl.ds(p * DP, DP)])
-
     def col_wait():
         for copy in col_in:
             copy.wait_recv()
 
-    def gathered(u):
-        for p in range(PARTS[u]):
-            gather_wait(u, 4, p)
-
     f = functools.partial
     early, late = ORDER[:5], ORDER[5:]
     plan = (
-        (Z, 0, ((f(gelu, 0, 0),), (f(gelu, 7, 0),), (f(gelu, 1, 0),), (f(gelu, 2, 0),))),
-        (Z, 1, ((col_wait, f(gelu, 0, 1)), (f(gelu, 7, 1),), (f(gelu, 1, 1),), (wait_wo, f(grad_pre, 0, 0)))),
-        (Z, 2, ((f(grad_pre, 0, 1),), (f(gelu, 6, 0), f(gelu, 6, 1)), (f(gelu, 2, 1), f(gelu, 5, 0)), (f(grad_pre, 7, 0),))),
-        (A, 0, ((f(grad_pre, 7, 1),), (f(gelu, 5, 1), f(gelu, 3, 0)))),
-        (Z, 3, ((f(gelu, 3, 1),), (f(gelu, 4, 0),), (f(gelu, 4, 1),), (f(grad_pre, 1, 0),))),
-        (Z, 4, ((f(grad_pre, 1, 1),), (transpose_w,), (f(grad_h, 0),), (f(grad_pre, 2, 0),))),
-        (A, 1, ((f(grad_pre, 2, 1),), (f(grad_pre, 6, 0),))),
-        (B, 0, ((f(grad_pre, 6, 1),), (f(grad_h, 6),))),
-        (A, 2, ((f(gathered, Z), f(grad_w, 0, 1, ORDER[:4], True)), (f(grad_w, 0, 1, ORDER[4:], False), f(w_sib, 0)))),
-        (B, 1, ((f(grad_w, 0, 0, ORDER[:4], True),), (f(grad_w, 0, 0, ORDER[4:], False),))),
-        (A, 3, ((f(grad_pre, 5, 0),), (f(grad_pre, 5, 1),))),
-        (B, 2, ((f(w_x, 0), f(grad_pre, 3, 0)), (f(grad_pre, 3, 1),))),
-        (A, 4, ((f(grad_pre, 4, 0),), (f(grad_pre, 4, 1), acc_send))),
-        (B, 3, ((f(grad_h, 5), f(grad_h, 3)), (f(grad_h, 4), f(grad_h, 2)))),
-        (R, 4, (
-            (f(grad_w, 1, 1, early, True),), (f(grad_w, 1, 0, early, True),),
-            (f(gathered, A), f(grad_w, 1, 1, late, False), f(w_sib, 1)),
-            (f(grad_w, 1, 0, late, False), f(v_part, 1, 1), f(v_part, 1, 0)),
-        )),
-        (B, 4, ((f(w_x, 1), f(w_h, 0)), (f(grad_w, 2, 1, early, True),))),
-        (R, 3, (
-            (f(grad_w, 2, 0, early, True),), (f(grad_h, 1),),
-            (f(gathered, B), f(grad_w, 2, 1, late, False), f(w_sib, 2)),
-            (f(grad_w, 2, 0, late, False), f(v_part, 2, 1), f(v_part, 2, 0)),
-        )),
-        (R, 2, ((f(w_x, 2), f(v_pair, 0, co)), (f(grad_h, 7), acc_end), (f(w_all, 0), f(v_sum, 0), f(v_pair, 1, yo)), ())),
-        (R, 1, ((f(w_h, 1), f(v_sum, 1), f(v_send, 0)), (), (f(v_wait, 0), f(v_send, 1)), (f(w_h, 2),))),
-        (R, 0, ((f(w_all, 1), f(v_wait, 1), f(v_send, 2)), (f(w_end, 0),), (f(w_all, 2), f(v_wait, 2), f(v_send, 3)), ())),
+        (Z, 0, 0, f(pre_send, 7), f(gelu, 0, 0)),
+        (Z, 0, 1, f(w_send, 0), f(gelu, 7, 0)),
+        (Z, 0, 2, f(pre_send, 1), f(gelu, 1, 0)),
+        (Z, 0, 3, f(pre_send, 2), f(gelu, 2, 0)),
+        (Z, 1, 0, f(pre_send, 6), col_wait, f(gelu, 0, 1)),
+        (Z, 1, 1, f(w_send, 1), f(gelu, 7, 1)),
+        (Z, 1, 2, f(pre_send, 5), f(gelu, 1, 1)),
+        (Z, 1, 3, wait_wo, f(grad_pre, 0, 0)),
+        (Z, 2, 0, f(pre_send, 3), f(grad_pre, 0, 1)),
+        (Z, 2, 1, f(pre_send, 4), f(gelu, 6, 0), f(gelu, 6, 1)),
+        (Z, 2, 2, f(gelu, 2, 1), f(gelu, 5, 0)),
+        (Z, 2, 3, f(grad_pre, 7, 0)),
+        (A, 0, 0, f(grad_pre, 7, 1)),
+        (A, 0, 1, f(gelu, 5, 1), f(gelu, 3, 0)),
+        (Z, 3, 0, f(gelu, 3, 1)),
+        (Z, 3, 1, f(gelu, 4, 0)),
+        (Z, 3, 2, f(gelu, 4, 1)),
+        (Z, 3, 3, f(grad_pre, 1, 0)),
+        (Z, 4, 0, f(grad_pre, 1, 1)),
+        (Z, 4, 1, f(grad_w, 0, 1, ORDER[:3], True)),
+        (Z, 4, 2, f(grad_w, 0, 0, ORDER[:3], True)),
+        (Z, 4, 3, f(grad_pre, 2, 0)),
+        (A, 1, 0, transpose_w, f(grad_pre, 2, 1)),
+        (A, 1, 1, f(grad_w, 0, 1, (2, 6), False)),
+        (B, 0, 0, f(grad_w, 0, 1, late, False), f(w_sib, 0)),
+        (B, 0, 1, f(grad_w, 0, 0, (2, 6, *late), False)),
+        (A, 2, 0, f(grad_pre, 6, 0)),
+        (A, 2, 1, f(w_x, 0), f(grad_pre, 6, 1)),
+        (B, 1, 0, f(grad_pre, 5, 0)),
+        (B, 1, 1, f(grad_pre, 5, 1)),
+        (A, 3, 0, f(grad_pre, 3, 0)),
+        (A, 3, 1, f(grad_pre, 3, 1)),
+        (B, 2, 0, f(grad_pre, 4, 0)),
+        (B, 2, 1, f(grad_pre, 4, 1), acc_send),
+        (A, 4, 0, f(grad_h, 4), f(grad_h, 7)),
+        (A, 4, 1, f(grad_h, 5), f(grad_h, 3)),
+        (B, 3, 0, f(grad_w, 1, 1, early, True)),
+        (B, 3, 1, f(w_h, 0), f(grad_w, 1, 0, early, True)),
+        (R, 5, 0, f(grad_h, 2)),
+        (R, 5, 1, f(grad_w, 1, 1, late, False), f(w_sib, 1)),
+        (R, 5, 2, f(grad_w, 1, 0, late, False), f(v_part, 1, 1)),
+        (R, 5, 3, f(v_part, 1, 0), f(grad_h, 6)),
+        (R, 4, 0, f(w_x, 1)),
+        (R, 4, 1, f(grad_h, 1)),
+        (B, 4, 0),
+        (B, 4, 1, f(grad_w, 2, 1, early, True)),
+        (R, 4, 2, f(w_all, 0), f(grad_w, 2, 0, early, True)),
+        (R, 4, 3, f(grad_h, 0)),
+        (R, 3, 0, f(grad_w, 2, 1, late, False), f(w_sib, 2)),
+        (R, 3, 1, f(grad_w, 2, 0, late, False), f(v_part, 2, 1), f(v_part, 2, 0)),
+        (R, 3, 2, f(w_x, 2), f(v_pair, 0, co)),
+        (R, 3, 3, f(w_h, 1)),
+        (R, 2, 0, f(v_sum, 0), f(v_pair, 1, yo)),
+        (R, 2, 1, acc_end),
+        (R, 2, 2),
+        (R, 2, 3, f(w_all, 1)),
+        (R, 1, 0, f(v_sum, 1), v_send),
+        (R, 1, 1),
+        (R, 1, 2, f(w_h, 2)),
+        (R, 1, 3),
+        (R, 0, 0),
+        (R, 0, 1, f(w_end, 0)),
+        (R, 0, 2),
+        (R, 0, 3, f(w_all, 2), v_end, f(w_end, 1)),
     )
-    for n, (u, step, work) in enumerate(plan):
-        for p in range(PARTS[u]):
-            if u == R:
-                if step < 4:
-                    sum_wait(step + 1, p)
-                sum_send(step, p)
-            elif n:
-                if step:
-                    gather_wait(u, step - 1, p)
-                gather_send(u, step, p)
-            for job in work[p]:
-                job()
-    w_end(1)
-    v_wait(3)
-    v_end()
+    marks = [len(sent)]
+    for n, (u, step, p, *work) in enumerate(plan):
+        if u == R:
+            sum_send(step, p)
+        elif n >= PARTS[Z]:
+            gather_send(u, step, p)
+        for job in work:
+            job()
+        marks.append(len(sent))
+        if n >= 16:
+            for copy in sent[marks[n - 16]:marks[n - 15]]:
+                copy.wait_send()
     for p in range(PARTS[R]):
-        sum_wait(0, p)
-    for j in range(D // 128):
-        cs = pl.ds(j * 128, 128)
-        t = slope[0, cs, pl.ds(0, TB)]
         for k in range(3):
-            t += rbuf[k, cs].astype(F32)
-        gx_ref[:, cs] = t.T * ri_ref[:, cs]
+            need(R, k, p)
+        at, size = SUM_ROWS[p]
+        for j in range(at, at + size, 128):
+            cs = pl.ds(j, 128)
+            t = slope[0, cs, pl.ds(0, TB)]
+            for k in range(3):
+                t += rbuf[k, cs].astype(F32)
+            gx_ref[:, cs] = t.T * ri_ref[:, cs]
+    for copy in (*sent[:marks[0]], *sent[marks[len(plan) - 16]:]):
+        copy.wait_send()
     w_end(2)
-    for copy in sent:
-        copy.wait_send()
 
 
 def finish(gx, gw, gri, gsi, gro, gso, gx_out, gwi_out, gwo_out, gri_out, gsi_out, gro_out, gso_out):
     gwo_out[...] = gw[0].astype(F32) * WSCALE
     gwi_out[...] = gw[1].astype(F32) * WSCALE
+    gx_out[...] = gx[...]
 
     @pl.when(pl.program_id(0) == 0)
     def _():
-        for src, dst in ((gx, gx_out), (gri, gri_out), (gsi, gsi_out), (gro, gro_out), (gso, gso_out)):
+        for src, dst in ((gri, gri_out), (gsi, gsi_out), (gro, gro_out), (gso, gso_out)):
             dst[...] = src[...]
 
 
@@ -428,9 +487,11 @@
     outs = pl.pallas_call(
         kernel,
         out_shape=[jax.ShapeDtypeStruct(shape, dtype) for shape, dtype in shapes],
-        in_specs=[vm, vm, vm, hbm, vm, hbm, hbm, vm, vm, vm, vm],
+        in_specs=[hbm, hbm, vm, hbm, hbm, hbm, hbm, vm, vm, vm, vm],
         out_specs=[vm] * 6,
         scratch_shapes=[
+            *[pltpu.VMEM((TB, D), BF)] * 3,
+            dma((3,)),
             pltpu.VMEM((FB, D), F32),
             pltpu.VMEM((FB, D), F32),
             pltpu.VMEM((NZ, NF, 2 * TB), BF),
@@ -456,9 +517,9 @@
             pltpu.VMEM((2, 3, 128, D), BF),
             pltpu.VMEM((2, 2, 128, D), BF),
             pltpu.VMEM((2, 4, 128, D), BF),
-            pltpu.VMEM((2, 8, D), F32),
-            pltpu.VMEM((2, 8, D), F32),
-            pltpu.VMEM((NZ, 8, D), F32),
+            pltpu.VMEM((2, 16, 128), F32),
+            pltpu.VMEM((2, 16, 128), F32),
+            pltpu.VMEM((NZ, 16, 128), F32),
             dma((4, 15, 4)), dma((4, 15, 4)),
             dma((NZ, 2)), dma((NZ, 2)), dma((NZ, 2)),
             dma((2,)), dma((2,)), dma((2,)),
@@ -469,19 +530,16 @@
             dma((3,)), dma((3,)),
             dma((3, 3)), dma((3, 3)),
             dma((2,)), dma((2,)),
-            dma((2, 4)), dma((2, 4)),
+            dma((7,)), dma((7,)),
         ],
         compiler_params=pltpu.CompilerParams(
             collective_id=0, has_side_effects=True, vmem_limit_bytes=63 * 2**20
         ),
     )(inputs[0], cotangent[0], counts, pre_hidden[0], pre_out[0], w_in, w_out, r_in, s_in, r_out, s_out)
     steps = 3
-
-    def whole(shape):
-        return pl.BlockSpec(shape, lambda i: (0,) * len(shape))
-
     rows = pl.BlockSpec((FB // steps, D), lambda i: (i, 0))
-    small = [whole(shape) for shape, _ in shapes[2:]]
+    some = pl.BlockSpec((TB // 2, D), lambda i: (jnp.minimum(i, 1), 0))
+    small = [pl.BlockSpec(shape, lambda i: (0, 0)) for shape, _ in shapes[2:]]
     gx, gwi, gwo, gri, gsi, gro, gso = pl.pallas_call(
         finish,
         grid=(steps,),
@@ -489,8 +547,8 @@
             jax.ShapeDtypeStruct(shape, F32)
             for shape in ((TB, D), (FB, D), (FB, D), (1, D), (1, FB), (1, FB), (1, D))
         ],
-        in_specs=[whole((TB, D)), pl.BlockSpec((2, FB // steps, D), lambda i: (0, i, 0)), *small],
-        out_specs=[whole((TB, D)), rows, rows, *small],
+        in_specs=[some, pl.BlockSpec((2, FB // steps, D), lambda i: (0, i, 0)), *small],
+        out_specs=[some, rows, rows, *small],
         compiler_params=pltpu.CompilerParams(vmem_limit_bytes=63 * 2**20),
     )(*outs)
     return gx[None], gwi, gwo, gri, gsi, gro, gso

time: 113 us -> 108 us (0.956)
  Pallas kernels: 110 us -> 106 us
    pallas_call x1, Pallas kernels: 106 us -> 102 us  [per_device(): pl.pallas_call(kernel, out_shape=[jax.ShapeDtypeStruct(shape, dtype) for...]
where the time goes in v3:
time: 108 us; the launch traced here: 107 us
  Pallas kernels  106 us (98%)
    pallas_call x1, Pallas kernels, per_device(): pl.pallas_call(kernel, out_shape=[jax.ShapeDtypeStruct(shape, dtype) for...  102 us
    pallas_call x1, Pallas kernels, per_device(): pl.pallas_call(finish, grid=(steps,), out_shape=[jax.ShapeDtypeStruct(sha...  4.09 us

profile of v3, /device:TPU:16, one launch (start us, length us, event | category | flops | bytes accessed | tf_op | source)
XLA Modules:
  0.0 106.9 jit_solution(14148839850318095477)
XLA Ops:
  0.6 102.0 %shard_map.162 = (f32[128,896]{1,0:T(8,128)}, bf16[2,480,896]{2,1,0:T(8,128)(2,1)}, f32[1,896]{1,0:T(1,128)}, f32[1,480]{1,0:T(1,128)}, f32[1,480]{1,0:T(1,128)}, /*index=5*/f32[1,896]{1,0:T(1,128)}) custom-call(bf16[128,896]{1,0:T(8,128)(2,1)} %bitcast.6, bf16[128,896]{1,0:T(8,128)(2,1)} %bitcast.7, s32[1,128]{1,0:T(1,128)} %cnt_ref.1, ...), custom_call_target="tpu_custom_call" | custom-call | tf_op jit(solution)/shard_map/pallas_call | solution.py:487
  102.6 4.1 %shard_map.163 = (f32[128,896]{1,0:T(8,128)}, f32[480,896]{1,0:T(8,128)}, f32[480,896]{1,0:T(8,128)}, f32[1,896]{1,0:T(1,128)}, f32[1,480]{1,0:T(1,128)}, /*index=5*/f32[1,480]{1,0:T(1,128)}, f32[1,896]{1,0:T(1,128)}) custom-call(f32[128,896]{1,0:T(8,128)} %get-tuple-element.20.gx, bf16[2,480,896]{2,1,0:T(8,128)(2,1)} %get-tuple-element.21.gw, ...), custom_call_target="tpu_custom_call" | custom-call | tf_op jit(solution)/shard_map/pallas_call | solution.py:543

commit v4 on v3

--- a/solution.py
+++ b/solution.py
@@ -357,7 +357,11 @@
 
     def sum_send(step, p):
         rows = pl.ds(*SUM_ROWS[p])
-        hops = (*HOPS[:14], LAST[p])
+        hops = [*HOPS[:14], LAST[p]]
+        if p == 0:
+            hops[5] = (0, (0, 1), (7, 1))
+        if p == 1:
+            hops[8] = (1, (0, 1), (1, 1))
         for k in SUM_STEPS[step]:
             way, _, (ds, dr) = hops[k]
             t = slope[ds, rows, pl.ds(dr * TB, TB)]

time: 108 us -> 107 us (level)
  no operation moved by 1% of the time
where the time goes in v4:
time: 107 us
  Pallas kernels  106 us (99%)
    pallas_call x1, Pallas kernels, per_device(): pl.pallas_call(kernel, out_shape=[jax.ShapeDtypeStruct(shape, dtype) for...  102 us
    pallas_call x1, Pallas kernels, per_device(): pl.pallas_call(finish, grid=(steps,), out_shape=[jax.ShapeDtypeStruct(sha...  4.09 us

profile of v4, /device:TPU:16, one launch (start us, length us, event | category | flops | bytes accessed | tf_op | source)
XLA Modules:
  0.0 107.0 jit_solution(442431041259542779)
XLA Ops:
  0.6 102.1 %shard_map.162 = (f32[128,896]{1,0:T(8,128)}, bf16[2,480,896]{2,1,0:T(8,128)(2,1)}, f32[1,896]{1,0:T(1,128)}, f32[1,480]{1,0:T(1,128)}, f32[1,480]{1,0:T(1,128)}, /*index=5*/f32[1,896]{1,0:T(1,128)}) custom-call(bf16[128,896]{1,0:T(8,128)(2,1)} %bitcast.6, bf16[128,896]{1,0:T(8,128)(2,1)} %bitcast.7, s32[1,128]{1,0:T(1,128)} %cnt_ref.1, ...), custom_call_target="tpu_custom_call" | custom-call | tf_op jit(solution)/shard_map/pallas_call | solution.py:491
  102.7 4.1 %shard_map.163 = (f32[128,896]{1,0:T(8,128)}, f32[480,896]{1,0:T(8,128)}, f32[480,896]{1,0:T(8,128)}, f32[1,896]{1,0:T(1,128)}, f32[1,480]{1,0:T(1,128)}, /*index=5*/f32[1,480]{1,0:T(1,128)}, f32[1,896]{1,0:T(1,128)}) custom-call(f32[128,896]{1,0:T(8,128)} %get-tuple-element.20.gx, bf16[2,480,896]{2,1,0:T(8,128)(2,1)} %get-tuple-element.21.gw, ...), custom_call_target="tpu_custom_call" | custom-call | tf_op jit(solution)/shard_map/pallas_call | solution.py:547
